TPU v7x, 32 devices: a whole 2x2x4 slice. The times are simulated.
32 devices in a mesh: dp: 4 (over y, core), seq: 8 (over z, x).
Axes of the slice: x: 2, y: 2, z: 4, core: 2. Of those that a mesh axis runs over, the one named last changes fastest.
Arguments:
- inputs: bfloat16 [16384, 1024], P(('dp', 'seq')), may hold values from -6 to 6
- text_state: bfloat16 [8, 128, 1024], replicated, may hold values from -6 to 6
- text_segment: int32 [8, 128], replicated, may hold values from 0 to 3, never falling along the last dimension, each value on 1 to 64 neighbouring positions
- image_text: int32 [16], replicated, may hold values from 0 to 7
- image_segment: int32 [16], replicated, may hold values from 0 to 3
- self_gain: float32 [1024], replicated, may hold values from 0.5 to 1.5
- self_shift: float32 [1024], replicated, may hold values from -1.5 to 1.5
- qkv_weight: bfloat16 [1024, 3072], replicated, may hold values from -0.1875 to 0.1875
- self_weight: bfloat16 [1024, 1024], replicated, may hold values from -0.75 to 0.75
- cross_gain: float32 [1024], replicated, may hold values from 0.5 to 1.5
- cross_shift: float32 [1024], replicated, may hold values from -1.5 to 1.5
- query_weight: bfloat16 [1024, 1024], replicated, may hold values from -0.1875 to 0.1875
- text_weight: bfloat16 [1024, 2048], replicated, may hold values from -0.1875 to 0.1875
- cross_weight: bfloat16 [1024, 1024], replicated, may hold values from -0.75 to 0.75
- feed_gain: float32 [1024], replicated, may hold values from 0.5 to 1.5
- feed_shift: float32 [1024], replicated, may hold values from -1.5 to 1.5
- up_weight: bfloat16 [1024, 4096], replicated, may hold values from -0.1875 to 0.1875
- down_weight: bfloat16 [4096, 1024], replicated, may hold values from -0.09375 to 0.09375
- cotangent: bfloat16 [16384, 1024], P(('dp', 'seq')), may hold values from -6 to 6
Outputs:
- output: bfloat16 [16384, 1024], P(('dp', 'seq'))
- input_grad: float32 [16384, 1024], P(('dp', 'seq'))
- text_grad: float32 [8, 128, 1024], replicated
- self_gain_grad: float32 [1024], P('seq')
- self_shift_grad: float32 [1024], P('seq')
- qkv_weight_grad: float32 [1024, 3072], P('seq')
- self_weight_grad: float32 [1024, 1024], P('seq')
- cross_gain_grad: float32 [1024], P('seq')
- cross_shift_grad: float32 [1024], P('seq')
- query_weight_grad: float32 [1024, 1024], P('seq')
- text_weight_grad: float32 [1024, 2048], P('seq')
- cross_weight_grad: float32 [1024, 1024], P('seq')
- feed_gain_grad: float32 [1024], P('seq')
- feed_shift_grad: float32 [1024], P('seq')
- up_weight_grad: float32 [1024, 4096], P('seq')
- down_weight_grad: float32 [4096, 1024], P('seq')
All inputs are finite; a program needn't handle non-finite values.
Results may differ from a plain program's by a relative error of at most 0.024.
Values may be sent and summed in bfloat16 or wider, within the bound.
No kernel may reach another device: no remote copies, remote signals or barrier semaphores. Data moves between devices by JAX's collectives and lax.ppermute only.
A program may use at most 320 MiB of HBM per device.

v0:
```python
import math

import jax
import jax.numpy as jnp
from jax import lax
from jax.sharding import PartitionSpec as P

D = 1024
HEADS = 16
HEAD = 64
TEXT_LEN = 128
IMG_TOK = 1024


NEGATIVE = -1e30
EPSILON = 1e-05


def shifted(block, axis, distance):
    devices = range(lax.axis_size(axis))
    route = [(i - distance, i) for i in devices if i - distance in devices]
    return lax.ppermute(block, axis, route)


def layer_norm(values, gain, shift):
    average = jnp.mean(values, axis=-1, keepdims=True)
    centered = values - average
    inverse = lax.rsqrt(jnp.mean(centered * centered, axis=-1, keepdims=True) + EPSILON)
    return centered * inverse * gain + shift


def norm_back(values, gain, shift, upstream):
    _, pullback = jax.vjp(layer_norm, values, gain, shift)
    return pullback(upstream)


def gelu_fn(pre_act):
    return jax.nn.gelu(pre_act, approximate=True)


def body(
    inputs,
    text_state,
    text_segment,
    image_text,
    image_segment,
    self_gain,
    self_shift,
    qkv_weight,
    self_weight,
    cross_gain,
    cross_shift,
    query_weight,
    text_weight,
    cross_weight,
    feed_gain,
    feed_shift,
    up_weight,
    down_weight,
    cotangent,
):
    rows_here = inputs.shape[0]
    score_scale = 1.0 / math.sqrt(HEAD)
    shards = lax.axis_size("seq")
    my_index = lax.axis_index("seq")
    group_id = lax.axis_index("dp")
    img_group = image_text.shape[0] // lax.axis_size("dp")
    rows_group = lax.dynamic_slice_in_dim(image_text, group_id * img_group, img_group, 0)
    segs_group = lax.dynamic_slice_in_dim(image_segment, group_id * img_group, img_group, 0)
    image_slots = jnp.arange(img_group, dtype=jnp.int32)
    own_start = my_index * rows_here
    q_pos = own_start + jnp.arange(rows_here, dtype=jnp.int32)
    q_img = q_pos // IMG_TOK
    image_first = q_img[0] * IMG_TOK
    resid = inputs.astype(jnp.float32)
    act_one = layer_norm(resid, self_gain, self_shift).astype(jnp.bfloat16)
    qkv_low = jnp.dot(act_one, qkv_weight, preferred_element_type=jnp.float32).astype(jnp.bfloat16)
    queries = qkv_low[:, :D].reshape(rows_here, HEADS, HEAD)
    pairs = qkv_low[:, D:]

    def block_needed(block_start):
        return block_start >= image_first

    def block_scores(key_block, block_start):
        block_rows = key_block.shape[0]
        key_heads = key_block[:, :D].reshape(block_rows, HEADS, HEAD)
        value_heads = key_block[:, D:].reshape(block_rows, HEADS, HEAD)
        k_pos = block_start + jnp.arange(block_rows, dtype=jnp.int32)
        k_img = k_pos // IMG_TOK
        scores = (
            jnp.einsum("qhd,khd->hqk", queries, key_heads, preferred_element_type=jnp.float32)
            * score_scale
        )
        allowed = (
            (k_img[None, :] == q_img[:, None])
            & (k_pos[None, :] <= q_pos[:, None])
            & (k_pos[None, :] >= 0)
        )
        return (jnp.where(allowed[None], scores, NEGATIVE), allowed, key_heads, value_heads)

    def fold_keys(running, key_block, block_start):

        def fold_compute(state):
            summed, row_top, row_total = state
            scores, allowed, key_heads, value_heads = block_scores(key_block, block_start)
            new_top = jnp.maximum(row_top, jnp.max(scores, axis=2))
            weights = jnp.where(allowed[None], jnp.exp(scores - new_top[:, :, None]), 0.0)
            factor = jnp.exp(row_top - new_top)
            part_sum = jnp.einsum(
                "hqk,khd->qhd",
                weights.astype(jnp.bfloat16),
                value_heads,
                preferred_element_type=jnp.float32,
            )
            return (
                summed * factor.T[:, :, None] + part_sum,
                new_top,
                row_total * factor + jnp.sum(weights, axis=2),
            )

        def fold_skip(state):
            return state

        return lax.cond(block_needed(block_start), fold_compute, fold_skip, running)

    initial = (
        jnp.zeros((rows_here, HEADS, HEAD), jnp.float32),
        jnp.full((HEADS, rows_here), NEGATIVE, jnp.float32),
        jnp.zeros((HEADS, rows_here), jnp.float32),
    )
    folded = fold_keys(initial, pairs, own_start)
    earlier = []
    step = 1
    neighbour = shifted(pairs, "seq", step)
    earlier.append(neighbour)
    folded = fold_keys(folded, neighbour, own_start - step * rows_here)
    summed, row_top, row_total = folded
    attn_heads = summed / row_total.T[:, :, None]
    log_total = row_top + jnp.log(row_total)
    attended_low = attn_heads.reshape(rows_here, D).astype(jnp.bfloat16)
    mid_one = resid + jnp.dot(attended_low, self_weight, preferred_element_type=jnp.float32)
    act_two = layer_norm(mid_one, cross_gain, cross_shift).astype(jnp.bfloat16)
    cross_q = (
        jnp.dot(act_two, query_weight, preferred_element_type=jnp.float32)
        .astype(jnp.bfloat16)
        .reshape(rows_here, HEADS, HEAD)
    )
    text_keys = text_state.shape[0] * text_state.shape[1]
    text_flat = text_state.reshape(text_keys, D)
    text_kv = jnp.dot(text_flat, text_weight, preferred_element_type=jnp.float32).astype(
        jnp.bfloat16
    )
    text_k = text_kv[:, :D].reshape(text_keys, HEADS, HEAD)
    text_v = text_kv[:, D:].reshape(text_keys, HEADS, HEAD)
    local_img = q_img - (q_img[0] - q_img[0])
    onehot = (local_img[:, None] == image_slots[None, :]).astype(jnp.int32)
    tok_row = jnp.sum(onehot * rows_group[None, :], axis=1)
    tok_seg = jnp.sum(onehot * segs_group[None, :], axis=1)
    key_row = jnp.arange(text_keys, dtype=jnp.int32) // TEXT_LEN
    key_seg = text_segment.reshape(-1)
    cross_allowed = (key_row[None, :] == tok_row[:, None]) & (key_seg[None, :] == tok_seg[:, None])
    cross_scores = (
        jnp.einsum("qhd,khd->hqk", cross_q, text_k, preferred_element_type=jnp.float32)
        * score_scale
    )
    cross_probs = jax.nn.softmax(jnp.where(cross_allowed[None], cross_scores, NEGATIVE), axis=-1)
    cross_low = cross_probs.astype(jnp.bfloat16)
    crossed_low = (
        jnp.einsum("hqk,khd->qhd", cross_low, text_v, preferred_element_type=jnp.float32)
        .astype(jnp.bfloat16)
        .reshape(rows_here, D)
    )
    mid_two = mid_one + jnp.dot(crossed_low, cross_weight, preferred_element_type=jnp.float32)
    act_three = layer_norm(mid_two, feed_gain, feed_shift).astype(jnp.bfloat16)
    pre_act = jnp.dot(act_three, up_weight, preferred_element_type=jnp.float32)
    hidden_low = gelu_fn(pre_act).astype(jnp.bfloat16)
    output = (
        mid_two + jnp.dot(hidden_low, down_weight, preferred_element_type=jnp.float32)
    ).astype(jnp.bfloat16)
    upstream = cotangent.astype(jnp.float32)
    grad_three = upstream.astype(jnp.bfloat16)
    d_down = jnp.einsum("tf,td->fd", hidden_low, grad_three, preferred_element_type=jnp.float32)
    d_hidden = jnp.einsum("td,fd->tf", grad_three, down_weight, preferred_element_type=jnp.float32)
    _, gelu_pull = jax.vjp(gelu_fn, pre_act)
    d_pre = gelu_pull(d_hidden)[0].astype(jnp.bfloat16)
    d_up = jnp.einsum("td,tf->df", act_three, d_pre, preferred_element_type=jnp.float32)
    d_act_three = jnp.einsum("tf,df->td", d_pre, up_weight, preferred_element_type=jnp.float32)
    d_norm_three, d_feed_gain, d_feed_shift = norm_back(mid_two, feed_gain, feed_shift, d_act_three)
    d_mid_two = upstream + d_norm_three
    grad_two = d_mid_two.astype(jnp.bfloat16)
    d_cross_w = jnp.einsum("td,te->de", crossed_low, grad_two, preferred_element_type=jnp.float32)
    d_crossed = (
        jnp.einsum("te,de->td", grad_two, cross_weight, preferred_element_type=jnp.float32)
        .astype(jnp.bfloat16)
        .reshape(rows_here, HEADS, HEAD)
    )
    d_text_v = jnp.einsum("hqk,qhd->khd", cross_low, d_crossed, preferred_element_type=jnp.float32)
    d_cross_p = jnp.einsum("qhd,khd->hqk", d_crossed, text_v, preferred_element_type=jnp.float32)
    d_cross_s = (
        cross_probs * (d_cross_p - jnp.sum(cross_probs * d_cross_p, axis=-1, keepdims=True))
    ).astype(jnp.bfloat16)
    d_cross_q = (
        (
            jnp.einsum("hqk,khd->qhd", d_cross_s, text_k, preferred_element_type=jnp.float32)
            * score_scale
        )
        .reshape(rows_here, D)
        .astype(jnp.bfloat16)
    )
    d_text_k = (
        jnp.einsum("hqk,qhd->khd", d_cross_s, cross_q, preferred_element_type=jnp.float32)
        * score_scale
    )
    text_term = jnp.concatenate(
        [d_text_k.reshape(text_keys, D), d_text_v.reshape(text_keys, D)], axis=1
    )
    text_total = lax.psum(text_term, ("dp", "seq"))
    text_low = text_total.astype(jnp.bfloat16)
    text_grad = jnp.einsum(
        "ke,de->kd", text_low, text_weight, preferred_element_type=jnp.float32
    ).reshape(text_state.shape)
    col_part = D // shards
    text_cols = lax.dynamic_slice_in_dim(text_flat, my_index * col_part, col_part, 1)
    d_text_w = jnp.einsum("kd,ke->de", text_cols, text_low, preferred_element_type=jnp.float32)
    d_query_w = jnp.einsum("td,te->de", act_two, d_cross_q, preferred_element_type=jnp.float32)
    d_act_two = jnp.einsum("te,de->td", d_cross_q, query_weight, preferred_element_type=jnp.float32)
    d_norm_two, d_cross_gain, d_cross_shift = norm_back(mid_one, cross_gain, cross_shift, d_act_two)
    d_mid_one = d_mid_two + d_norm_two
    grad_one = d_mid_one.astype(jnp.bfloat16)
    d_self_w = jnp.einsum("td,te->de", attended_low, grad_one, preferred_element_type=jnp.float32)
    d_attn = (
        jnp.einsum("te,de->td", grad_one, self_weight, preferred_element_type=jnp.float32)
        .astype(jnp.bfloat16)
        .reshape(rows_here, HEADS, HEAD)
    )
    row_delta = jnp.einsum("qhd,qhd->hq", d_attn.astype(jnp.float32), attn_heads)
    sources = [shifted(pairs, "seq", 1)]

    def block_grads(key_block, block_start, d_running):

        def block_compute(d_state):
            scores, allowed, key_heads, value_heads = block_scores(key_block, block_start)
            softmax_w = jnp.where(allowed[None], jnp.exp(scores - log_total[:, :, None]), 0.0)
            d_values = jnp.einsum(
                "hqk,qhd->khd",
                softmax_w.astype(jnp.bfloat16),
                d_attn,
                preferred_element_type=jnp.float32,
            )
            d_probs = jnp.einsum(
                "qhd,khd->hqk", d_attn, value_heads, preferred_element_type=jnp.float32
            )
            d_scores = (softmax_w * (d_probs - row_delta[:, :, None])).astype(jnp.bfloat16)
            d_next = (
                d_state
                + jnp.einsum(
                    "hqk,khd->qhd", d_scores, key_heads, preferred_element_type=jnp.float32
                )
                * score_scale
            )
            d_keys = (
                jnp.einsum("hqk,qhd->khd", d_scores, queries, preferred_element_type=jnp.float32)
                * score_scale
            )
            return (
                d_next,
                jnp.concatenate(
                    [d_keys.reshape(rows_here, D), d_values.reshape(rows_here, D)], axis=1
                ),
            )

        def block_skip(d_state):
            return (d_state, jnp.zeros((rows_here, 2 * D), jnp.float32))

        return lax.cond(block_needed(block_start), block_compute, block_skip, d_running)

    d_queries, home_grad = block_grads(
        pairs, own_start, jnp.zeros((rows_here, HEADS, HEAD), jnp.float32)
    )
    step = 1
    d_queries, d_pair = block_grads(sources[step - 1], own_start - step * rows_here, d_queries)
    home_grad = home_grad + shifted(d_pair.astype(jnp.bfloat16), "seq", -step).astype(d_pair.dtype)
    d_qkv = jnp.concatenate([d_queries.reshape(rows_here, D), home_grad], axis=1).astype(
        jnp.bfloat16
    )
    d_qkv_w = jnp.einsum("td,te->de", act_one, d_qkv, preferred_element_type=jnp.float32)
    d_act_one = jnp.einsum("te,de->td", d_qkv, qkv_weight, preferred_element_type=jnp.float32)
    d_norm_one, d_self_gain, d_self_shift = norm_back(resid, self_gain, self_shift, d_act_one)
    input_grad = d_mid_one + d_norm_one
    reduced = (
        lax.psum(
            lax.psum_scatter(
                d_self_gain.astype(jnp.bfloat16), "seq", scatter_dimension=0, tiled=True
            ),
            "dp",
        ).astype(jnp.float32),
        lax.psum(
            lax.psum_scatter(
                d_self_shift.astype(jnp.bfloat16), "seq", scatter_dimension=0, tiled=True
            ),
            "dp",
        ).astype(jnp.float32),
        lax.psum(
            lax.psum_scatter(d_qkv_w.astype(jnp.bfloat16), "seq", scatter_dimension=0, tiled=True),
            "dp",
        ).astype(jnp.float32),
        lax.psum(
            lax.psum_scatter(d_self_w.astype(jnp.bfloat16), "seq", scatter_dimension=0, tiled=True),
            "dp",
        ).astype(jnp.float32),
        lax.psum(
            lax.psum_scatter(
                d_cross_gain.astype(jnp.bfloat16), "seq", scatter_dimension=0, tiled=True
            ),
            "dp",
        ).astype(jnp.float32),
        lax.psum(
            lax.psum_scatter(
                d_cross_shift.astype(jnp.bfloat16), "seq", scatter_dimension=0, tiled=True
            ),
            "dp",
        ).astype(jnp.float32),
        lax.psum(
            lax.psum_scatter(
                d_query_w.astype(jnp.bfloat16), "seq", scatter_dimension=0, tiled=True
            ),
            "dp",
        ).astype(jnp.float32),
        lax.psum(
            lax.psum_scatter(
                d_cross_w.astype(jnp.bfloat16), "seq", scatter_dimension=0, tiled=True
            ),
            "dp",
        ).astype(jnp.float32),
        lax.psum(
            lax.psum_scatter(
                d_feed_gain.astype(jnp.bfloat16), "seq", scatter_dimension=0, tiled=True
            ),
            "dp",
        ).astype(jnp.float32),
        lax.psum(
            lax.psum_scatter(
                d_feed_shift.astype(jnp.bfloat16), "seq", scatter_dimension=0, tiled=True
            ),
            "dp",
        ).astype(jnp.float32),
        lax.psum(
            lax.psum_scatter(d_up.astype(jnp.bfloat16), "seq", scatter_dimension=0, tiled=True),
            "dp",
        ).astype(jnp.float32),
        lax.psum(
            lax.psum_scatter(d_down.astype(jnp.bfloat16), "seq", scatter_dimension=0, tiled=True),
            "dp",
        ).astype(jnp.float32),
    )
    return (
        output,
        input_grad,
        text_grad,
        reduced[0],
        reduced[1],
        reduced[2],
        reduced[3],
        reduced[4],
        reduced[5],
        reduced[6],
        d_text_w,
        reduced[7],
        reduced[8],
        reduced[9],
        reduced[10],
        reduced[11],
    )


def solution(mesh):
    placed = (
        P(("dp", "seq"), None),
        P(),
        P(),
        P(),
        P(),
        P(),
        P(),
        P(),
        P(),
        P(),
        P(),
        P(),
        P(),
        P(),
        P(),
        P(),
        P(),
        P(),
        P(("dp", "seq"), None),
    )
    return jax.shard_map(
        body,
        mesh=mesh,
        in_specs=placed,
        out_specs=(
            P(("dp", "seq"), None),
            P(("dp", "seq"), None),
            P(),
            P("seq"),
            P("seq"),
            P("seq", None),
            P("seq", None),
            P("seq"),
            P("seq"),
            P("seq", None),
            P("seq", None),
            P("seq", None),
            P("seq"),
            P("seq"),
            P("seq", None),
            P("seq", None),
        ),
        check_vma=False,
    )
```

profile of v0, /device:TPU:0, one launch (start us, length us, event | category | flops | bytes accessed | tf_op | source)
XLA Modules:
  0.0 1012.3 jit_solution(8162966890436952901)
XLA Ops:
  11.0 6.7 convolution_convert_fusion.3
  19.3 6.1 collective-permute-start
  29.4 7.3 convolution_convert_fusion.4
  47.0 21.6 %conditional.4 = (f32[512,16,64]{0,2,1:T(8,128)}, f32[16,512]{1,0:T(8,128)}, f32[16,512]{1,0:T(8,128)S(1)}) conditional(s32[]{:T(128)} %convert_element_type.185, () %tuple.48, (s32[]{:T(128)}, s32[512]{0:T(512)S(1)}, s32[512]{0:T(512)S(1)}, bf16[512,2048]{1,0:T(8,128)(2,1)}, bf16[512,16,64]{0,2,1:T(8,128)(2,1)S(1)}) %tuple.136), branch_computations={%region_2.3_spmd, %region_3.6_spmd} | conditional | flops 1129882624 | bytes 65385504 | solution.py:124
  61.9 6.0 bitcast_add_fusion
  70.0 11.5 %fusion.129 = f32[512,4096]{1,0:T(8,128)} fusion(bf16[512,1024]{1,0:T(8,128)(2,1)} %param.45, bf16[4096,1024]{1,0:T(8,128)(2,1)} %param.44), kind=kOutput, calls=%fused_computation.236 | convolution fusion | flops 4294967296 | bytes 17825792 | tf_op jit(solution)/shard_map/td,fd->tf/dot_general | solution.py:183
  93.1 19.2 %fusion.125 = (f32[16,512]{1,0:T(8,128)S(1)}, f32[16,512,1024]{2,1,0:T(8,128)}) fusion(pred[512,1024]{1,0:T(8,128)(4,1)} %compare_and_fusion, bf16[512,16,64]{0,2,1:T(8,128)(2,1)S(1)} %bitcast.145, bf16[1024,16,64]{0,2,1:T(8,128)(2,1)} %bitcast.142), kind=kOutput, calls=%fused_computation.232 | convolution fusion | flops 1107297280 | bytes 37257216 | tf_op jit(solution)/shard_map/sub | solution.py:166
  112.3 13.9 %fusion.88 = bf16[16,64,512]{2,1,0:T(8,128)(2,1)S(1)} fusion(bf16[1024,16,64]{0,2,1:T(8,128)(2,1)} %bitcast.154, f32[16,512,1024]{2,1,0:T(8,128)} %get-tuple-element.355, f32[16,512]{1,0:T(8,128)S(1)} %get-tuple-element.354), kind=kOutput, calls=%fused_computation.170 | convolution fusion | flops 1091043328 | bytes 36732928 | tf_op jit(solution)/shard_map/hqk,khd->qhd/dot_general | solution.py:169
  130.7 15.7 %fusion.66 = (bf16[512,4096]{1,0:T(8,128)(2,1)S(1)}, f32[512,4096]{1,0:T(8,128)}) fusion(f32[512,4096]{1,0:T(8,128)} %fusion.129, bf16[1024,4096]{1,0:T(8,128)(2,1)} %param.43, f32[512,1024]{1,0:T(8,128)S(1)} %get-tuple-element.357, f32[1024]{0:T(1024)S(1)} %copy-done.68, f32[1024]{0:T(1024)S(1)} %copy-done.58, f32[512]{0:T(512)S(1)} %fusion.104, ...), kind=kOutput, calls=%fused_computation.113 | convolution fusion | flops 4339531776 | bytes 31469568 | tf_op jit(solution)/shard_map/dot_general | solution.py:175
  164.4 22.7 %multiply_reduce_fusion = (f32[16,512]{1,0:T(8,128)S(1)}, f32[16,512,1024]{2,1,0:T(8,128)}) fusion(f32[16,512,1024]{2,1,0:T(8,128)} %get-tuple-element.355, f32[16,512]{1,0:T(8,128)S(1)} %get-tuple-element.354, bf16[512,16,64]{0,2,1:T(8,128)(2,1)} %bitcast.161, bf16[1024,16,64]{0,2,1:T(8,128)(2,1)} %bitcast.155), kind=kOutput, calls=%fused_computation.97 | convolution fusion | flops 1098899456 | bytes 70320128 | tf_op jit(solution)/shard_map/qhd,khd->hqk/dot_general | solution.py:198
  187.1 28.0 %multiply_convert_fusion.2 = bf16[16,512,1024]{2,1,0:T(8,128)(2,1)} fusion(f32[16,512,1024]{2,1,0:T(8,128)} %get-tuple-element.362, f32[16,512]{1,0:T(8,128)S(1)} %get-tuple-element.361, f32[16,512,1024]{2,1,0:T(8,128)} %get-tuple-element.355, f32[16,512]{1,0:T(8,128)S(1)} %get-tuple-element.354), kind=kLoop, calls=%fused_computation.96 | loop fusion | flops 33554432 | bytes 83951616 | tf_op jit(solution)/shard_map/convert_element_type | solution.py:201
  215.1 12.8 %multiply_convert_fusion.4 = bf16[16,64,512]{2,1,0:T(8,128)(2,1)} fusion(bf16[1024,16,64]{0,2,1:T(8,128)(2,1)} %bitcast.143, bf16[16,512,1024]{2,1,0:T(8,128)(2,1)} %multiply_convert_fusion.2), kind=kOutput, calls=%fused_computation.156 | convolution fusion | flops 1074790400 | bytes 19922944 | tf_op jit(solution)/shard_map/hqk,khd->qhd/dot_general | solution.py:204
  254.5 38.7 %conditional.6 = (f32[512,16,64]{0,2,1:T(8,128)}, f32[512,2048]{0,1:T(8,128)}) conditional(s32[]{:T(128)} %convert_element_type.185, () %tuple.51, (s32[]{:T(128)}, s32[512]{0:T(512)S(1)}, s32[512]{0:T(512)S(1)}, bf16[512,2048]{1,0:T(8,128)(2,1)}, bf16[512,16,64]{0,2,1:T(8,128)(2,1)S(1)}, /*index=5*/f32[16,512]{1,0:T(8,128)S(1)}, ...), branch_computations={%region_23.24_spmd, %region_24.25_spmd} | conditional | flops 2737841152 | bytes 194884784 | solution.py:275
  269.6 6.0 fusion.18
  275.6 9.8 multiply_convert_fusion
  294.9 6.7 collective-permute-start.1
  303.3 102.5 %collective-permute-done.1 = bf16[512,2048]{0,1:T(8,128)(2,1)S(1)} collective-permute-done((bf16[512,2048]{0,1:T(8,128)(2,1)}, bf16[512,2048]{0,1:T(8,128)(2,1)S(1)}, u32[]{:S(2)}, u32[]{:S(2)}) %collective-permute-start.1) | collective-permute-done | bytes 2097184 | tf_op jit(solution)/shard_map/ppermute | solution.py:22
  410.3 7.1 convolution_convert_fusion.2
  417.5 12.8 %convolution_convert_fusion = bf16[4096,1024]{1,0:T(8,128)(2,1)} fusion(bf16[512,1024]{1,0:T(8,128)(2,1)} %param.45, f32[512,4096]{1,0:T(8,128)} %get-tuple-element.359), kind=kOutput, calls=%fused_computation.120 | convolution fusion | flops 4318035968 | bytes 17825792 | tf_op jit(solution)/shard_map/tf,td->fd/dot_general | solution.py:182
  431.0 10.8 %convolution_convert_fusion.1 = bf16[1024,4096]{1,0:T(8,128)(2,1)} fusion(bf16[512,4096]{1,0:T(8,128)(2,1)} %copy-done.75, f32[512,1024]{1,0:T(8,128)} %copy-done.14, f32[1024]{0:T(1024)S(1)} %copy-done.69, f32[1024]{0:T(1024)S(1)} %copy-done.59, f32[512]{0:T(512)S(1)} %copy-done.52, f32[512]{0:T(512)S(1)} %copy-done.43), kind=kOutput, calls=%fused_computation.121 | convolution fusion | flops 4301783040 | bytes 14692352 | tf_op jit(solution)/shard_map/td,tf->df/dot_general | solution.py:186
  443.8 11.7 %convolution_multiply_fusion.2 = f32[16,64,1024]{2,1,0:T(8,128)} fusion(bf16[512,16,64]{0,2,1:T(8,128)(2,1)} %bitcast.146, bf16[16,512,1024]{2,1,0:T(8,128)(2,1)} %multiply_convert_fusion.2), kind=kOutput, calls=%fused_computation.139 | convolution fusion | flops 1074790400 | bytes 22020096 | tf_op jit(solution)/shard_map/hqk,qhd->khd/dot_general | solution.py:211
  455.5 14.8 %fusion.67 = f32[16,64,1024]{2,1,0:T(8,128)} fusion(bf16[512,16,64]{0,2,1:T(8,128)(2,1)S(1)} %bitcast.162, f32[16,512,1024]{2,1,0:T(8,128)} %get-tuple-element.355, f32[16,512]{1,0:T(8,128)S(1)} %get-tuple-element.354), kind=kOutput, calls=%fused_computation.116 | convolution fusion | flops 1090519040 | bytes 38830080 | tf_op jit(solution)/shard_map/hqk,qhd->khd/dot_general | solution.py:197
  470.3 8.6 pad_maximum_fusion.2
  478.9 231.1 %all-reduce.13 = bf16[1024,2048]{0,1:T(8,128)(2,1)} all-reduce(f32[1024,2048]{0,1:T(8,128)} %pad_maximum_fusion.2), channel_id=1, replica_groups=mesh['dp'=4,'seq'=8] {'dp','seq'}, use_global_device_ids=true, to_apply=%region_29.30 | all-reduce | flops 2097152 | bytes 12582912 | tf_op jit(solution)/shard_map/psum | solution.py:217
  714.9 8.8 fusion.130
  723.8 6.2 add_convert_fusion.1
  730.0 32.4 %reduce-scatter.17.cloned.1.call-done = bf16[512,1024]{1,0:T(8,128)(2,1)} async-done(((bf16[4096,1024]{1,0:T(8,128)(2,1)}), bf16[512,1024]{1,0:T(8,128)(2,1)}) %reduce-scatter.17.cloned.1.call-update) | async-done | bytes 1048592 | tf_op jit(solution)/shard_map/reduce_scatter | solution.py:352
  762.4 151.9 %reduce-scatter.15.cloned.1.call-done = bf16[128,4096]{1,0:T(8,128)(2,1)} async-done(((bf16[1024,4096]{1,0:T(8,128)(2,1)}), bf16[128,4096]{1,0:T(8,128)(2,1)}) %reduce-scatter.15.cloned.1.call-update) | async-done | bytes 1048592 | tf_op jit(solution)/shard_map/reduce_scatter | solution.py:348
  914.4 7.5 fusion.116
  924.2 35.1 %all-reduce.6 = (bf16[1024]{0:T(1024)(128)(2,1)S(1)}, bf16[1024]{0:T(1024)(128)(2,1)S(1)}, bf16[1024]{0:T(1024)(128)(2,1)S(1)}, bf16[1024]{0:T(1024)(128)(2,1)S(...) all-reduce(bf16[1024]{0:T(1024)(128)(2,1)S(1)} %get-tuple-element.2, ...), channel_id=2, replica_groups=mesh['dp'=4,'seq'=8] {'seq'}, use_global_device_ids=true, to_apply=%region_31.32.clone | all-reduce | flops 6144 | bytes 24576
  959.8 6.1 all-reduce.7
  973.3 20.8 %all-reduce.12.cloned.1.call-done = (bf16[128,3072]{1,0:T(8,128)(2,1)}, bf16[128,1024]{1,0:T(8,128)(2,1)}, bf16[128,1024]{1,0:T(8,128)(2,1)}, bf16[128,1024]{1,0...) async-done(((bf16[128,3072]{1,0:T(8,128)(2,1)}, bf16[128,1024]{1,0:T(8,128)(2,1)}, bf16[128,1024]{1,0:T(8,128)(2,1)}, bf16[128,1024]{1,0:T(8,128)(2,1)}, ...) | async-done | bytes 3670032 | tf_op jit(solution)/shard_map/psum | solution.py:303
  (274 shorter events, 156.1 us)
Async XLA Ops:
  7.2 22.2 %copy-start = (bf16[8,128,1024]{2,1,0:T(8,128)(2,1)S(1)}, bf16[8,128,1024]{2,1,0:T(8,128)(2,1)}, u32[]{:S(2)}) copy-start(bf16[8,128,1024]{2,1,0:T(8,128)(2,1)} %param.28) | copy-start | bytes 6291460
  7.2 722.8 %reduce-scatter.13.cloned.1.call-start = ((), (), s32[]{:S(2)}) async-start(), calls=%async_computation.9 | async-start | bytes 2359296 | tf_op jit(solution)/shard_map/reduce_scatter | solution.py:330
  19.3 62.3 %collective-permute-start = (bf16[512,2048]{1,0:T(8,128)(2,1)}, bf16[512,2048]{1,0:T(8,128)(2,1)}, u32[]{:S(2)}, u32[]{:S(2)}) collective-permute-start(bf16[512,2048]{1,0:T(8,128)(2,1)} %slice.56), channel_id=1, source_target_pairs={{0,1},{1,2},{2,3},{3,4},{4,5},{5,6},{6,7},{8,9},{9,10},{10,11},{11... | collective-permute-start | bytes 6291464 | tf_op jit(solution)/shard_map/ppermute | solution.py:22
  26.5 55.1 %copy-start.34 = (s32[512]{0:T(512)}, s32[512]{0:T(512)S(1)}, u32[]{:S(2)}) copy-start(s32[512]{0:T(512)S(1)} %get-tuple-element.365) | copy-start | bytes 6148
  26.5 55.1 %copy-start.36 = (s32[512]{0:T(512)}, s32[512]{0:T(512)S(1)}, u32[]{:S(2)}) copy-start(s32[512]{0:T(512)S(1)} %get-tuple-element.366) | copy-start | bytes 6148
  29.4 52.2 %copy-start.1 = (bf16[512,1024]{0,1:T(8,128)(2,1)}, bf16[512,1024]{0,1:T(8,128)(2,1)S(1)}, u32[]{:S(2)}) copy-start(bf16[512,1024]{0,1:T(8,128)(2,1)S(1)} %copy.81) | copy-start | bytes 3145732
  47.0 21.7 %copy-start.55 = (s32[8,128]{1,0:T(8,128)S(1)}, s32[8,128]{1,0:T(8,128)}, u32[]{:S(2)}) copy-start(s32[8,128]{1,0:T(8,128)} %param.29) | copy-start | bytes 12292
  93.1 19.2 %copy-start.17 = (bf16[512,1024]{0,1:T(8,128)(2,1)}, bf16[512,1024]{0,1:T(8,128)(2,1)S(1)}, u32[]{:S(2)}) copy-start(bf16[512,1024]{0,1:T(8,128)(2,1)S(1)} %copy.85) | copy-start | bytes 3145732
  126.3 20.1 %slice-start = ((s8[8388608]{0:T(1024)(128)(4,1)}), s8[4194304]{0:T(1024)(128)(4,1)S(1)}, s32[]{:S(2)}) async-start(s8[8388608]{0:T(1024)(128)(4,1)} %bitcast.171), calls=%async_computation.13 | async-start | bytes 8388608
  130.2 21.7 %copy-start.14 = (f32[512,1024]{1,0:T(8,128)}, f32[512,1024]{1,0:T(8,128)S(1)}, u32[]{:S(2)}) copy-start(f32[512,1024]{1,0:T(8,128)S(1)} %get-tuple-element.357) | copy-start | bytes 6291460
  130.3 21.7 %copy-start.42 = (f32[512]{0:T(512)}, f32[512]{0:T(512)S(1)}, u32[]{:S(2)}) copy-start(f32[512]{0:T(512)S(1)} %broadcast_multiply_fusion) | copy-start | bytes 6148
  130.7 21.3 %copy-start.51 = (f32[512]{0:T(512)}, f32[512]{0:T(512)S(1)}, u32[]{:S(2)}) copy-start(f32[512]{0:T(512)S(1)} %fusion.104) | copy-start | bytes 6148
  130.7 15.7 %slice-start.1 = ((s8[8388608]{0:T(1024)(128)(4,1)}), s8[4194304]{0:T(1024)(128)(4,1)S(1)}, s32[]{:S(2)}) async-start(s8[8388608]{0:T(1024)(128)(4,1)} %bitcast.171), calls=%async_computation.14 | async-start | bytes 8388608
  164.3 565.7 %reduce-scatter.11.cloned.1.call-start = ((), (), s32[]{:S(2)}) async-start(), calls=%async_computation.8 | async-start | bytes 2359296 | tf_op jit(solution)/shard_map/reduce_scatter | solution.py:324
  215.1 12.8 %copy-start.45 = (f32[512]{0:T(512)S(1)}, f32[512]{0:T(512)}, u32[]{:S(2)}) copy-start(f32[512]{0:T(512)} %copy-done.44) | copy-start | bytes 6148
  215.1 12.8 %copy-start.54 = (f32[512]{0:T(512)S(1)}, f32[512]{0:T(512)}, u32[]{:S(2)}) copy-start(f32[512]{0:T(512)} %copy-done.53) | copy-start | bytes 6148
  215.1 12.8 %copy-start.57 = (f32[1024]{0:T(1024)S(1)}, f32[1024]{0:T(1024)}, u32[]{:S(2)}) copy-start(f32[1024]{0:T(1024)} %param.36) | copy-start | bytes 12292
  215.1 12.8 %copy-start.66 = (f32[1024]{0:T(1024)S(1)}, f32[1024]{0:T(1024)}, u32[]{:S(2)}) copy-start(f32[1024]{0:T(1024)} %param.37) | copy-start | bytes 12292
  232.6 497.4 %reduce-scatter.9.cloned.1.call-start = ((), (), s32[]{:S(2)}) async-start(), calls=%async_computation.7 | async-start | bytes 2359296 | tf_op jit(solution)/shard_map/reduce_scatter | solution.py:308
  244.1 485.9 %reduce-scatter.7.cloned.1.call-start = ((), (), s32[]{:S(2)}) async-start(), calls=%async_computation.6 | async-start | bytes 7077888 | tf_op jit(solution)/shard_map/reduce_scatter | solution.py:304
  294.9 111.0 %collective-permute-start.1 = (bf16[512,2048]{0,1:T(8,128)(2,1)}, bf16[512,2048]{0,1:T(8,128)(2,1)S(1)}, u32[]{:S(2)}, u32[]{:S(2)}) collective-permute-start(bf16[512,2048]{0,1:T(8,128)(2,1)} %get-tuple-element.146), channel_id=1, source_target_pairs={{1,0},{2,1},{3,2},{4,3},{5,4},{6,5},{7,6},{9,8},{10,9},{11,10},{12... | collective-permute-start | bytes 6291464 | tf_op jit(solution)/shard_map/ppermute | solution.py:22
  303.3 105.7 %copy-start.26 = (bf16[512,16,64]{0,2,1:T(8,128)(2,1)}, bf16[512,16,64]{0,2,1:T(8,128)(2,1)S(1)}, u32[]{:S(2)}) copy-start(bf16[512,16,64]{0,2,1:T(8,128)(2,1)S(1)} %convert.7) | copy-start | bytes 3145732
  417.4 345.0 %reduce-scatter.17.cloned.1.call-start = ((), (), s32[]{:S(2)}) async-start(), calls=%async_computation.11 | async-start | bytes 9437184 | tf_op jit(solution)/shard_map/reduce_scatter | solution.py:352
  430.4 483.9 %reduce-scatter.15.cloned.1.call-start = ((), (), s32[]{:S(2)}) async-start(), calls=%async_computation.10 | async-start | bytes 9437184 | tf_op jit(solution)/shard_map/reduce_scatter | solution.py:348
  441.9 552.2 %all-reduce.12.cloned.1.call-start = ((), (), s32[]{:S(2)}) async-start(), calls=%async_computation.12 | async-start | bytes 7340032 | tf_op jit(solution)/shard_map/psum | solution.py:303
  443.8 11.8 %copy-start.29 = (bf16[512,1024]{0,1:T(8,128)(2,1)S(1)}, bf16[512,1024]{0,1:T(8,128)(2,1)}, u32[]{:S(2)}) copy-start(bf16[512,1024]{0,1:T(8,128)(2,1)} %copy.87) | copy-start | bytes 3145732
  710.0 13.7 %slice-start.2 = ((s8[8388608]{0:T(1024)(128)(4,1)}), s8[4194304]{0:T(1024)(128)(4,1)S(1)}, s32[]{:S(2)}) async-start(s8[8388608]{0:T(1024)(128)(4,1)} %bitcast.173), calls=%async_computation.15 | async-start | bytes 8388608
  710.0 13.7 %slice-start.4 = ((s8[8388608]{0:T(1024)(128)(4,1)}), s8[4194304]{0:T(1024)(128)(4,1)S(1)}, s32[]{:S(2)}) async-start(s8[8388608]{0:T(1024)(128)(4,1)} %bitcast.178), calls=%async_computation.17 | async-start | bytes 8388608
  914.3 9.9 copy-start.60
  914.3 9.9 copy-start.61
  914.4 9.9 copy-start.62
  914.4 9.9 copy-start.63
  (56 other events, 234.5 us)
Sparse Core Ops, SparseCore 0:
  164.5 88.9 reduce-scatter.12
  257.0 66.9 reduce-scatter.10
  327.5 109.9 reduce-scatter.8
  440.9 143.7 reduce-scatter.6
  588.1 174.2 reduce-scatter.16
  766.3 147.9 reduce-scatter.14
  917.1 77.0 all-reduce.11
where the time goes:
time: 1020 us; the launch traced here: 1010 us
  waiting for transfers between devices  308 us (30%)
  blocking collectives  272 us (27%)
  matrix products  266 us (26%)
  other arithmetic  82.7 us (8%)
  local copies, waits for them, and re-layouts  52.5 us (5%)
  between operations  16.5 us (2%)
  starting transfers between devices  13.9 us (1%)
    psum x1, blocking collectives, body(): text_total = lax.psum(text_term, ('dp', 'seq'))  231 us
    reduce_scatter x1, waiting for transfers between devices, body(): lax.psum_scatter(d_up.astype(jnp.bfloat16), 'seq', scatter_dimension=0, t...  152 us
    ppermute x2, waiting for transfers between devices, shifted(): return lax.ppermute(block, axis, route)  102 us
    unnamed x1, blocking collectives  35.1 us
    reduce_scatter x1, waiting for transfers between devices, body(): lax.psum_scatter(d_down.astype(jnp.bfloat16), 'seq', scatter_dimension=0,...  32.4 us
    convert_element_type x1, other arithmetic, body(): d_cross_s = (cross_probs * (d_cross_p - jnp.sum(cross_probs * d_cross_p,...  28 us
    dot_general x1, matrix products, body(): jnp.einsum('qhd,khd->hqk', d_crossed, text_v, preferred_element_type=jnp....  22.7 us
    psum x1, waiting for transfers between devices, body(): lax.psum(lax.psum_scatter(d_qkv_w.astype(jnp.bfloat16), 'seq', scatter_di...  20.8 us
  transfers between devices with their start and end apart: 9, of which 4 were waited for; matrix products, arithmetic and copies ran while one was open for 28% of the time, Pallas kernels for 0%

commit v1 on v0

v1 whole, which is shorter than its diff:
```python
import functools
import math

import jax
import jax.numpy as jnp
from jax import lax
from jax.experimental import pallas as pl
from jax.experimental.pallas import tpu as pltpu
from jax.sharding import PartitionSpec as P

D = 1024
HEADS = 16
HEAD = 64
FF = 4096
TEXT_LEN = 128
IMG_TOK = 1024
PAIR = 2 * HEAD
SCALE = 1.0 / math.sqrt(HEAD)

NEGATIVE = -1e30
EPSILON = 1e-05
BF = jnp.bfloat16
F32 = jnp.float32
NN = (((1,), (0,)), ((), ()))
NT = (((1,), (1,)), ((), ()))
TN = (((0,), (0,)), ((), ()))
VMEM_LIMIT = 56 * 1024 * 1024


def mm(a, b, dims=NN):
    return lax.dot_general(a, b, dims, preferred_element_type=F32)


def normed(values):
    average = jnp.mean(values, axis=-1, keepdims=True)
    centered = values - average
    inverse = lax.rsqrt(jnp.mean(centered * centered, axis=-1, keepdims=True) + EPSILON)
    return centered * inverse, inverse


def norm_back(normal, inverse, gain, upstream):
    w = upstream * gain
    along = jnp.mean(w * normal, axis=-1, keepdims=True)
    return inverse * (w - jnp.mean(w, axis=-1, keepdims=True) - normal * along)


def head_lanes(h):
    lane = lax.broadcasted_iota(jnp.int32, (1, PAIR), 1)
    return (lane >= h * HEAD) & (lane < (h + 1) * HEAD)


def only_head(block, h):
    return jnp.where(head_lanes(h), block, jnp.zeros_like(block))


def params(grid_dims=1):
    return pltpu.CompilerParams(
        dimension_semantics=("arbitrary",) * grid_dims, vmem_limit_bytes=VMEM_LIMIT
    )


def cost(flops, moved):
    return pl.CostEstimate(flops=int(flops), bytes_accessed=int(moved), transcendentals=0)


def whole(shape):
    zeros = (0,) * len(shape)
    return pl.BlockSpec(shape, lambda *_: zeros)


def shape_of(shape, dtype):
    return jax.ShapeDtypeStruct(shape, dtype)


def norm_project(x, gain, shift, weight, first_col, name):
    rows, width = x.shape
    cols = weight.shape[1] - first_col
    bn = 512

    def kernel(x_ref, gain_ref, shift_ref, w_ref, act_ref, out_ref):
        @pl.when(pl.program_id(0) == 0)
        def _():
            normal, _ = normed(x_ref[...].astype(F32))
            act_ref[...] = (normal * gain_ref[...] + shift_ref[...]).astype(BF)

        out_ref[...] = mm(act_ref[...], w_ref[...]).astype(BF)

    return pl.pallas_call(
        kernel,
        grid=(cols // bn,),
        in_specs=[
            whole((rows, width)),
            whole((1, width)),
            whole((1, width)),
            pl.BlockSpec((width, bn), lambda j: (0, first_col // bn + j)),
        ],
        out_specs=[whole((rows, width)), pl.BlockSpec((rows, bn), lambda j: (0, j))],
        out_shape=[shape_of((rows, width), BF), shape_of((rows, cols), BF)],
        compiler_params=params(),
        cost_estimate=cost(2 * rows * width * cols, 2 * width * cols + 4 * rows * width),
        name=name,
    )(x, gain, shift, weight)


def causal_forward(qkv):
    rows = qkv.shape[0]
    half = rows // 2
    pairs = D // PAIR

    def kernel(q_ref, k_ref, v_ref, out_ref, log_ref):
        for first in (0, half):
            keys = first + half
            q = q_ref[first:keys, :] * SCALE
            k = k_ref[:keys, :]
            v = v_ref[:keys, :]
            at_q = first + lax.broadcasted_iota(jnp.int32, (half, keys), 0)
            at_k = lax.broadcasted_iota(jnp.int32, (half, keys), 1)
            total = jnp.zeros((half, PAIR), F32)
            logs = jnp.zeros((half, PAIR), F32)
            for h in (0, 1):
                s = mm(q, only_head(k, h), NT)
                s = jnp.where(at_q >= at_k, s, NEGATIVE)
                top = jnp.max(s, axis=1, keepdims=True)
                p = jnp.exp(s - top)
                part = jnp.sum(p, axis=1, keepdims=True)
                total = total + mm(p.astype(BF), only_head(v, h)) * (1.0 / part)
                logs = jnp.where(head_lanes(h), top + jnp.log(part), logs)
            out_ref[first:keys, :] = total
            log_ref[first:keys, :] = logs

    block = (rows, PAIR)
    return pl.pallas_call(
        kernel,
        grid=(pairs,),
        in_specs=[
            pl.BlockSpec(block, lambda p: (0, p)),
            pl.BlockSpec(block, lambda p: (0, pairs + p)),
            pl.BlockSpec(block, lambda p: (0, 2 * pairs + p)),
        ],
        out_specs=[pl.BlockSpec(block, lambda p: (0, p))] * 2,
        out_shape=[shape_of((rows, D), F32)] * 2,
        compiler_params=params(),
        cost_estimate=cost(8 * rows * rows * D, 14 * rows * D),
        name="causal_forward",
    )(qkv, qkv, qkv)


def earlier_forward(odd, qkv, pairs_before, own_out, own_log):
    rows = qkv.shape[0]
    half = rows // 2
    pairs = D // PAIR

    def kernel(odd_ref, q_ref, k_ref, v_ref, own_ref, log_ref, out_ref, new_log_ref):
        @pl.when(odd_ref[0] == 0)
        def _():
            out_ref[...] = own_ref[...].astype(BF)
            new_log_ref[...] = log_ref[...]

        @pl.when(odd_ref[0] != 0)
        def _():
            for first in (0, half):
                span = slice(first, first + half)
                q = q_ref[span, :] * SCALE
                total = own_ref[span, :]
                logs = log_ref[span, :]
                result = jnp.zeros_like(total)
                new_logs = logs
                for h in (0, 1):
                    s = mm(q, only_head(k_ref[...], h), NT)
                    old = logs[:, h * HEAD : h * HEAD + 1]
                    top = jnp.maximum(old, jnp.max(s, axis=1, keepdims=True))
                    p = jnp.exp(s - top)
                    share = jnp.exp(old - top)
                    part = share + jnp.sum(p, axis=1, keepdims=True)
                    mixed = mm(p.astype(BF), only_head(v_ref[...], h))
                    mixed = mixed + only_head(total, h) * share
                    result = result + mixed * (1.0 / part)
                    new_logs = jnp.where(head_lanes(h), top + jnp.log(part), new_logs)
                out_ref[span, :] = result.astype(BF)
                new_log_ref[span, :] = new_logs

    block = (rows, PAIR)
    first = pl.BlockSpec(block, lambda p, odd: (0, p))
    second = pl.BlockSpec(block, lambda p, odd: (0, pairs + p))
    return pl.pallas_call(
        kernel,
        grid_spec=pltpu.PrefetchScalarGridSpec(
            num_scalar_prefetch=1,
            grid=(pairs,),
            in_specs=[first, first, second, first, first],
            out_specs=[first, first],
        ),
        out_shape=[shape_of((rows, D), BF), shape_of((rows, D), F32)],
        compiler_params=params(),
        cost_estimate=cost(8 * rows * rows * D, 18 * rows * D),
        name="earlier_forward",
    )(odd, qkv, pairs_before, pairs_before, own_out, own_log)


def cross_weights(keys, queries, bias):
    s = mm(keys, queries, NT) + bias
    p = jnp.exp(s - jnp.max(s, axis=0, keepdims=True))
    return p * (1.0 / jnp.sum(p, axis=0, keepdims=True))


def middle_forward(attended, x, self_w, query_w, cross_w, gains, text_kv, bias):
    rows = x.shape[0]
    tile = rows // 2

    def kernel(
        at_ref, x_ref, sw_ref, qw_ref, cw_ref, gains_ref, kv_ref, bias_ref,
        mid1_ref, act2_ref, cq_ref, crossed_ref, mid2_ref, act3_ref,
    ):
        mid1 = x_ref[...].astype(F32) + mm(at_ref[...], sw_ref[...])
        mid1_ref[...] = mid1
        normal, _ = normed(mid1)
        act2 = (normal * gains_ref[0:1, :] + gains_ref[1:2, :]).astype(BF)
        act2_ref[...] = act2
        cq_ref[...] = mm(act2, qw_ref[...]).astype(BF)
        bias_col = bias_ref[:, 0:1]
        for p in range(D // PAIR):
            span = slice(p * PAIR, (p + 1) * PAIR)
            q = cq_ref[:, span] * SCALE
            k = kv_ref[:, span]
            v = kv_ref[:, D + p * PAIR : D + (p + 1) * PAIR]
            total = jnp.zeros((tile, PAIR), F32)
            for h in (0, 1):
                w = cross_weights(only_head(k, h), q, bias_col)
                total = total + mm(w.astype(BF), only_head(v, h), TN)
            crossed_ref[:, span] = total.astype(BF)
        mid2 = mid1 + mm(crossed_ref[...], cw_ref[...])
        mid2_ref[...] = mid2
        normal, _ = normed(mid2)
        act3_ref[...] = (normal * gains_ref[2:3, :] + gains_ref[3:4, :]).astype(BF)

    row_block = pl.BlockSpec((tile, D), lambda i: (i, 0))
    square = whole((D, D))
    return pl.pallas_call(
        kernel,
        grid=(rows // tile,),
        in_specs=[
            row_block, row_block, square, square, square,
            whole(gains.shape), whole(text_kv.shape), whole(bias.shape),
        ],
        out_specs=[row_block] * 6,
        out_shape=[
            shape_of((rows, D), t) for t in (F32, BF, BF, BF, F32, BF)
        ],
        compiler_params=params(),
        cost_estimate=cost(8 * rows * D * D, 6 * D * D + 20 * rows * D),
        name="middle_forward",
    )(attended, x, self_w, query_w, cross_w, gains, text_kv, bias)


def feed_half(which, act3, grad3, up, down, shards, before):
    rows = act3.shape[0]
    bw = FF // (2 * shards)
    root = math.sqrt(2.0 / math.pi)

    def kernel(which_ref, a_ref, g_ref, up_ref, down_ref, *rest):
        if before is None:
            y_ref, dh_ref, da_ref = rest
        else:
            before_ref, y_ref, dh_ref, da_ref = rest
        h = mm(a_ref[...], up_ref[...])
        sq = h * h
        t = jnp.tanh(h * (root + (root * 0.044715) * sq))
        y_ref[...] = (0.5 * h * (1.0 + t)).astype(BF)
        slope = 0.5 * (1.0 + t) + (0.5 * h) * (1.0 - t * t) * (root + (3 * root * 0.044715) * sq)
        dy = mm(g_ref[...], down_ref[...], NT)
        dh = (dy * slope).astype(BF)
        dh_ref[...] = dh
        part = mm(dh, up_ref[...], NT)

        @pl.when(pl.program_id(0) == 0)
        def _():
            if before is None:
                da_ref[...] = part
            else:
                da_ref[...] = before_ref[...] + part

        @pl.when(pl.program_id(0) != 0)
        def _():
            da_ref[...] += part

    token = whole((rows, D))
    in_specs = [
        token,
        token,
        pl.BlockSpec((D, bw), lambda s, which: (0, 2 * s + which[0])),
        pl.BlockSpec((bw, D), lambda s, which: (2 * s + which[0], 0)),
    ]
    operands = [which, act3, grad3, up, down]
    if before is not None:
        in_specs.append(token)
        operands.append(before)
    return pl.pallas_call(
        kernel,
        grid_spec=pltpu.PrefetchScalarGridSpec(
            num_scalar_prefetch=1,
            grid=(shards,),
            in_specs=in_specs,
            out_specs=[pl.BlockSpec((rows, bw), lambda s, which: (0, s))] * 2 + [token],
        ),
        out_shape=[
            shape_of((rows, FF // 2), BF),
            shape_of((rows, FF // 2), BF),
            shape_of((rows, D), F32),
        ],
        compiler_params=params(),
        cost_estimate=cost(3 * rows * D * FF, 2 * D * FF + 8 * rows * D),
        name="feed_half",
    )(*operands)


def feed_output(own, mid2, hidden_own, hidden_other, down, shards):
    rows = mid2.shape[0]
    bw = FF // (2 * shards)

    def kernel(own_ref, mid_ref, a_ref, b_ref, da_ref, db_ref, out_ref, acc_ref):
        s = pl.program_id(0)
        part = mm(a_ref[...], da_ref[...]) + mm(b_ref[...], db_ref[...])

        @pl.when(s == 0)
        def _():
            acc_ref[...] = mid_ref[...] + part

        @pl.when(s != 0)
        def _():
            acc_ref[...] += part

        @pl.when(s == shards - 1)
        def _():
            out_ref[...] = acc_ref[...].astype(BF)

    token = whole((rows, D))
    hid = pl.BlockSpec((rows, bw), lambda s, own: (0, s))
    return pl.pallas_call(
        kernel,
        grid_spec=pltpu.PrefetchScalarGridSpec(
            num_scalar_prefetch=1,
            grid=(shards,),
            in_specs=[
                token,
                hid,
                hid,
                pl.BlockSpec((bw, D), lambda s, own: (2 * s + own[0], 0)),
                pl.BlockSpec((bw, D), lambda s, own: (2 * s + 1 - own[0], 0)),
            ],
            out_specs=token,
            scratch_shapes=[pltpu.VMEM((rows, D), F32)],
        ),
        out_shape=shape_of((rows, D), BF),
        compiler_params=params(),
        cost_estimate=cost(2 * rows * D * FF, 2 * D * FF + 14 * rows * D),
        name="feed_output",
    )(own, mid2, hidden_own, hidden_other, down, down)


def middle_backward(d_act3, mid2, upstream, mid1, cq, text_kv, bias, cross_w, query_w, self_w, gains):
    rows = mid2.shape[0]
    tile = rows // 2
    steps = rows // tile

    def kernel(
        da3_ref, mid2_ref, g_ref, mid1_ref, cq_ref, kv_ref, bias_ref, cw_ref, qw_ref, sw_ref, gains_ref,
        g2_ref, dcq_ref, dmid1_ref, g1_ref, dat_ref, dkv_ref, dgains_ref, kv_acc,
    ):
        i = pl.program_id(0)

        @pl.when(i == 0)
        def _():
            kv_acc[...] = jnp.zeros_like(kv_acc)
            dgains_ref[...] = jnp.zeros_like(dgains_ref)

        up3 = da3_ref[...]
        normal, inverse = normed(mid2_ref[...])
        dgains_ref[2:3, :] += jnp.sum(up3 * normal, axis=0, keepdims=True)
        dgains_ref[3:4, :] += jnp.sum(up3, axis=0, keepdims=True)
        dmid2 = g_ref[...].astype(F32) + norm_back(normal, inverse, gains_ref[2:3, :], up3)
        g2 = dmid2.astype(BF)
        g2_ref[...] = g2
        dat_ref[...] = mm(g2, cw_ref[...], NT).astype(BF)
        bias_col = bias_ref[:, 0:1]
        for p in range(D // PAIR):
            span = slice(p * PAIR, (p + 1) * PAIR)
            vspan = slice(D + p * PAIR, D + (p + 1) * PAIR)
            q = cq_ref[:, span] * SCALE
            dc = dat_ref[:, span]
            k = kv_ref[:, span]
            v = kv_ref[:, vspan]
            dq = jnp.zeros((tile, PAIR), F32)
            dk = jnp.zeros((TEXT_LEN, PAIR), F32)
            dv = jnp.zeros((TEXT_LEN, PAIR), F32)
            for h in (0, 1):
                kh = only_head(k, h)
                w = cross_weights(kh, q, bias_col)
                dw = mm(only_head(v, h), dc, NT)
                ds = (w * (dw - jnp.sum(w * dw, axis=0, keepdims=True))).astype(BF)
                dq = dq + mm(ds, kh, TN)
                dk = dk + mm(ds, only_head(q, h))
                dv = dv + mm(w.astype(BF), only_head(dc, h))
            dcq_ref[:, span] = (dq * SCALE).astype(BF)
            kv_acc[:, span] += dk
            kv_acc[:, vspan] += dv
        up2 = mm(dcq_ref[...], qw_ref[...], NT)
        normal, inverse = normed(mid1_ref[...])
        dgains_ref[0:1, :] += jnp.sum(up2 * normal, axis=0, keepdims=True)
        dgains_ref[1:2, :] += jnp.sum(up2, axis=0, keepdims=True)
        dmid1 = dmid2 + norm_back(normal, inverse, gains_ref[0:1, :], up2)
        dmid1_ref[...] = dmid1
        g1 = dmid1.astype(BF)
        g1_ref[...] = g1
        dat_ref[...] = mm(g1, sw_ref[...], NT).astype(BF)

        @pl.when(i == steps - 1)
        def _():
            dkv_ref[...] = kv_acc[...].astype(BF)

    row_block = pl.BlockSpec((tile, D), lambda i: (i, 0))
    square = whole((D, D))
    return pl.pallas_call(
        kernel,
        grid=(steps,),
        in_specs=[
            row_block, row_block, row_block, row_block, row_block,
            whole(text_kv.shape), whole(bias.shape), square, square, square, whole(gains.shape),
        ],
        out_specs=[row_block] * 5 + [whole(text_kv.shape), whole((8, D))],
        out_shape=[shape_of((rows, D), t) for t in (BF, BF, F32, BF, BF)]
        + [shape_of(text_kv.shape, BF), shape_of((8, D), F32)],
        scratch_shapes=[pltpu.VMEM(text_kv.shape, F32)],
        compiler_params=params(),
        cost_estimate=cost(10 * rows * D * D, 6 * D * D + 24 * rows * D),
        name="middle_backward",
    )(d_act3, mid2, upstream, mid1, cq, text_kv, bias, cross_w, query_w, self_w, gains)


def deltas_of(d_out, out):
    prod = d_out.astype(F32) * out.astype(F32)
    high = prod.astype(BF)
    low = (prod - high.astype(F32)).astype(BF)
    row = lax.broadcasted_iota(jnp.int32, (8, PAIR), 0)
    lane = lax.broadcasted_iota(jnp.int32, (8, PAIR), 1)
    pick = jnp.where(lane // HEAD == row, 1.0, 0.0).astype(BF)
    return mm(pick, high, NT) + mm(pick, low, NT)


def key_block_back(k, v, q, d_out, log_row, delta_row, h, masked_from=None):
    kh = only_head(k, h)
    s = mm(kh, q, NT)
    p = jnp.exp(s - log_row)
    if masked_from is not None:
        at_k = lax.broadcasted_iota(jnp.int32, s.shape, 0)
        at_q = lax.broadcasted_iota(jnp.int32, s.shape, 1) + masked_from
        p = jnp.where(at_q >= at_k, p, 0.0)
    dp = mm(only_head(v, h), d_out, NT)
    ds = (p * (dp - delta_row)).astype(BF)
    dv = mm(p.astype(BF), only_head(d_out, h))
    dk = mm(ds, only_head(q, h))
    dq = mm(ds, kh, TN)
    return dq, dk, dv


def earlier_backward(scalars, qkv, pairs_before, d_out, out, logs):
    rows = qkv.shape[0]
    half = rows // 2
    pairs = D // PAIR
    count = pairs // 2

    def kernel(sc_ref, q_ref, k_ref, v_ref, do_ref, out_ref, log_ref, dq_ref, dkv_ref):
        @pl.when(sc_ref[0] == 0)
        def _():
            dq_ref[...] = jnp.zeros_like(dq_ref)
            dkv_ref[...] = jnp.zeros_like(dkv_ref)

        @pl.when(sc_ref[0] != 0)
        def _():
            q = q_ref[...] * SCALE
            d_o = do_ref[...]
            deltas = deltas_of(d_o, out_ref[...])
            dq_total = jnp.zeros((rows, PAIR), F32)
            for first in (0, half):
                span = slice(first, first + half)
                dk_total = jnp.zeros((half, PAIR), F32)
                dv_total = jnp.zeros((half, PAIR), F32)
                for h in (0, 1):
                    dq, dk, dv = key_block_back(
                        k_ref[span, :], v_ref[span, :], q, d_o,
                        log_ref[0, h : h + 1, :], deltas[h : h + 1, :], h,
                    )
                    dq_total = dq_total + dq
                    dk_total = dk_total + dk
                    dv_total = dv_total + dv
                dkv_ref[0, span, :] = dk_total.astype(BF)
                dkv_ref[1, span, :] = dv_total.astype(BF)
            dq_ref[...] = dq_total

    block = (rows, PAIR)

    def at(offset):
        return pl.BlockSpec(block, lambda p, sc: (0, offset + sc[1] * count + p))

    return pl.pallas_call(
        kernel,
        grid_spec=pltpu.PrefetchScalarGridSpec(
            num_scalar_prefetch=1,
            grid=(count,),
            in_specs=[
                at(0),
                at(0),
                at(pairs),
                at(0),
                at(0),
                pl.BlockSpec((1, 2, rows), lambda p, sc: (sc[1] * count + p, 0, 0)),
            ],
            out_specs=[
                pl.BlockSpec(block, lambda p, sc: (0, p)),
                pl.BlockSpec((2, rows, PAIR), lambda p, sc: (0, 0, p)),
            ],
        ),
        out_shape=[shape_of((rows, D // 2), F32), shape_of((2, rows, D // 2), BF)],
        compiler_params=params(),
        cost_estimate=cost(10 * rows * rows * D, 10 * rows * D),
        name="earlier_backward",
    )(scalars, qkv, pairs_before, pairs_before, d_out, out, logs)


def causal_backward(scalars, qkv, d_out, out, logs, dq_before):
    rows = qkv.shape[0]
    half = rows // 2
    pairs = D // PAIR
    count = pairs // 2

    def kernel(sc_ref, q_ref, k_ref, v_ref, do_ref, out_ref, log_ref, before_ref, grads_ref):
        q = q_ref[...] * SCALE
        d_o = do_ref[...]
        deltas = deltas_of(d_o, out_ref[...])
        dq_late = before_ref[half:, :]
        dq_early = before_ref[:half, :]
        for first in (0, half):
            span = slice(first, first + half)
            dk_total = jnp.zeros((half, PAIR), F32)
            dv_total = jnp.zeros((half, PAIR), F32)
            for h in (0, 1):
                dq, dk, dv = key_block_back(
                    k_ref[span, :], v_ref[span, :], q[first:], d_o[first:],
                    log_ref[0, h : h + 1, first:], deltas[h : h + 1, first:], h, masked_from=0,
                )
                if first == 0:
                    dq_early = dq_early + dq[:half]
                    dq_late = dq_late + dq[half:]
                else:
                    dq_late = dq_late + dq
                dk_total = dk_total + dk
                dv_total = dv_total + dv
            grads_ref[1, span, :] = dk_total.astype(BF)
            grads_ref[2, span, :] = dv_total.astype(BF)
        grads_ref[0, :half, :] = (dq_early * SCALE).astype(BF)
        grads_ref[0, half:, :] = (dq_late * SCALE).astype(BF)

    block = (rows, PAIR)

    def at(offset):
        return pl.BlockSpec(block, lambda p, sc: (0, offset + sc[1] * count + p))

    return pl.pallas_call(
        kernel,
        grid_spec=pltpu.PrefetchScalarGridSpec(
            num_scalar_prefetch=1,
            grid=(count,),
            in_specs=[
                at(0),
                at(pairs),
                at(2 * pairs),
                at(0),
                at(0),
                pl.BlockSpec((1, 2, rows), lambda p, sc: (sc[1] * count + p, 0, 0)),
                pl.BlockSpec(block, lambda p, sc: (0, p)),
            ],
            out_specs=pl.BlockSpec((3, rows, PAIR), lambda p, sc: (0, 0, p)),
        ),
        out_shape=shape_of((3, rows, D // 2), BF),
        compiler_params=params(),
        cost_estimate=cost(10 * rows * rows * D, 14 * rows * D),
        name="causal_backward",
    )(scalars, qkv, qkv, qkv, d_out, out, logs, dq_before)


def project_back(own, grads_own, grads_other, weight, x, kinds, name):
    rows = x.shape[0]
    count, _, width = grads_own.shape
    first = 3 - count

    def kernel(own_ref, ga_ref, gb_ref, wa_ref, wb_ref, x_ref, out_ref, sums_ref, acc_ref):
        j = pl.program_id(0)
        part = mm(ga_ref[...], wa_ref[...], NT) + mm(gb_ref[...], wb_ref[...], NT)

        @pl.when(j == 0)
        def _():
            acc_ref[...] = part

        @pl.when(j != 0)
        def _():
            acc_ref[...] += part

        @pl.when(j == count - 1)
        def _():
            total = acc_ref[...]
            out_ref[...] = total.astype(kinds)
            normal, _ = normed(x_ref[...].astype(F32))
            sums_ref[...] = jnp.zeros_like(sums_ref)
            sums_ref[0:1, :] = jnp.sum(total * normal, axis=0, keepdims=True)
            sums_ref[1:2, :] = jnp.sum(total, axis=0, keepdims=True)

    grad = pl.BlockSpec((None, rows, width), lambda j, own: (j, 0, 0))
    return pl.pallas_call(
        kernel,
        grid_spec=pltpu.PrefetchScalarGridSpec(
            num_scalar_prefetch=1,
            grid=(count,),
            in_specs=[
                grad,
                grad,
                pl.BlockSpec((D, width), lambda j, own: (0, 2 * (first + j) + own[0])),
                pl.BlockSpec((D, width), lambda j, own: (0, 2 * (first + j) + 1 - own[0])),
                whole((rows, D)),
            ],
            out_specs=[whole((rows, D)), whole((8, D))],
            scratch_shapes=[pltpu.VMEM((rows, D), F32)],
        ),
        out_shape=[shape_of((rows, D), kinds), shape_of((8, D), F32)],
        compiler_params=params(),
        cost_estimate=cost(4 * rows * D * width * count, 4 * D * width * count + 8 * rows * D),
        name=name,
    )(own, grads_own, grads_other, weight, weight, x)


def input_back(d_act, d_act_other, x, d_mid1, gain):
    rows = x.shape[0]
    tile = rows // 4

    def kernel(da_ref, db_ref, x_ref, dm_ref, gain_ref, out_ref):
        normal, inverse = normed(x_ref[...].astype(F32))
        up = da_ref[...] + db_ref[...].astype(F32)
        out_ref[...] = dm_ref[...] + norm_back(normal, inverse, gain_ref[...], up)

    row_block = pl.BlockSpec((tile, D), lambda i: (i, 0))
    return pl.pallas_call(
        kernel,
        grid=(rows // tile,),
        in_specs=[row_block] * 4 + [whole((1, D))],
        out_specs=row_block,
        out_shape=shape_of((rows, D), F32),
        compiler_params=params(),
        cost_estimate=cost(20 * rows * D, 16 * rows * D),
        name="input_back",
    )(d_act, d_act_other, x, d_mid1, gain)


def weight_grad(scalars, lefts, rights, bw, split_rows, late=(), name="weight_grad"):
    n = len(lefts)
    rows = lefts[0].shape[1]
    tokens = [a.shape[0] for a in lefts]
    total = sum(tokens)
    three = rights[0].ndim == 3
    if three:
        parts, _, bn = rights[0].shape
        cols = parts * bn
    else:
        cols = rights[0].shape[1]
        bn = min(512, cols if split_rows else cols // 2)
    out_cols = cols if split_rows else cols // 2
    steps = out_cols // bn
    out_rows = rows // 2 if split_rows else rows
    blocks = rows // bw
    per_rhs = 1 if split_rows else 2

    def kernel(sc_ref, *refs):
        left_refs = refs[:n]
        right_refs = refs[n : n + n * per_rhs]
        send_ref, keep_ref, turned = refs[n + n * per_rhs :][:3]
        j = pl.program_id(0)

        @pl.when(j == 0)
        def _():
            start = 0
            for ref, t in zip(left_refs, tokens, strict=True):
                turned[:, start : start + t] = ref[...].T
                start += t

        def product(rhs_refs, lo):
            acc = None
            start = 0
            for place, (ref, t) in enumerate(zip(rhs_refs, tokens, strict=True)):
                if place not in late or True:
                    piece = mm(lo[:, start : start + t], ref[...])
                    if place in late:
                        piece = jnp.where(j > 0, piece, 0.0)
                    acc = piece if acc is None else acc + piece
                start += t
            return acc

        if split_rows:
            for b in range(blocks):
                at = pl.multiple_of(sc_ref[1 + b] * bw, bw)
                lo = turned[pl.ds(at, bw), :]
                target = send_ref if b < blocks // 2 else keep_ref
                place = (b % (blocks // 2)) * bw
                target[place : place + bw, :] = product(right_refs, lo).astype(BF)
        else:
            big = min(rows, 512)
            for b in range(rows // big):
                lo = turned[b * big : (b + 1) * big, :]
                span = slice(b * big, (b + 1) * big)
                send_ref[span, :] = product(right_refs[:n], lo).astype(BF)
                keep_ref[span, :] = product(right_refs[n:], lo).astype(BF)

    in_specs = [whole(a.shape) for a in lefts]
    operands = list(lefts)
    if split_rows:
        for place, r in enumerate(rights):
            t = tokens[place]
            if three and place in late:
                in_specs.append(
                    pl.BlockSpec((None, t, bn), lambda j, sc: (jnp.maximum(j - 1, 0), 0, 0))
                )
            elif three:
                in_specs.append(pl.BlockSpec((None, t, bn), lambda j, sc: (j, 0, 0)))
            else:
                in_specs.append(pl.BlockSpec((t, bn), lambda j, sc: (0, j)))
            operands.append(r)
    else:
        for kept in (0, 1):
            for place, r in enumerate(rights):
                t = tokens[place]
                if kept:
                    spec = pl.BlockSpec((t, bn), lambda j, sc: (0, (1 - sc[0]) * steps + j))
                else:
                    spec = pl.BlockSpec((t, bn), lambda j, sc: (0, sc[0] * steps + j))
                in_specs.append(spec)
                operands.append(r)
    return pl.pallas_call(
        kernel,
        grid_spec=pltpu.PrefetchScalarGridSpec(
            num_scalar_prefetch=1,
            grid=(steps,),
            in_specs=in_specs,
            out_specs=[pl.BlockSpec((out_rows, bn), lambda j, sc: (0, j))] * 2,
            scratch_shapes=[pltpu.VMEM((rows, total), BF)],
        ),
        out_shape=[shape_of((out_rows, out_cols), BF)] * 2,
        compiler_params=params(),
        cost_estimate=cost(
            2 * rows * total * cols, 2 * rows * cols + 2 * total * (rows + cols)
        ),
        name=name,
    )(scalars, *operands)


def swap(block, axis, bit):
    route = [(i, i ^ (1 << bit)) for i in range(lax.axis_size(axis))]
    return lax.ppermute(block, axis, route)


def pick(block, place, dim):
    return lax.dynamic_index_in_dim(block, place, dim, keepdims=False)


def bit_of(index, bit):
    return (index >> bit) & 1


def add(a, b):
    return (a.astype(F32) + b.astype(F32)).astype(BF)


class Reducer:
    def __init__(self):
        self.seq_bits = lax.axis_size("seq").bit_length() - 1
        self.dp_bits = lax.axis_size("dp").bit_length() - 1
        self.me = lax.axis_index("seq")
        self.dp = lax.axis_index("dp")

    def row_order(self, bit):
        count = 1 << self.seq_bits
        mine = bit_of(self.me, bit)
        sent, kept = [], []
        for s in range(count):
            if not (s >> bit) & 1:
                sent.append(s + (1 - mine) * (1 << bit))
                kept.append(s + mine * (1 << bit))
        return sent + kept

    def finish(self, block, seq_left, dp_left, order):
        seq_left = list(seq_left)
        for axis, bit in order:
            if axis == "seq":
                place = seq_left.index(bit)
                mine = bit_of(self.me, bit)
                sent, kept = pick(block, 1 - mine, place), pick(block, mine, place)
                seq_left.pop(place)
            else:
                mine = bit_of(self.dp, bit)
                place = len(seq_left)
                shape = block.shape
                block = block.reshape(shape[:place] + (2, shape[place] // 2) + shape[place + 1 :])
                sent, kept = pick(block, 1 - mine, place), pick(block, mine, place)
            block = add(kept, swap(sent, axis, bit))
        return block

    def gather(self, block, dp_steps):
        for bit, dim in reversed(dp_steps):
            other = swap(block, "dp", bit)
            mine = bit_of(self.dp, bit) == 0
            block = jnp.concatenate(
                [jnp.where(mine, block, other), jnp.where(mine, other, block)], axis=dim
            )
        return block

    def both_cores(self, block):
        other = swap(block, "dp", 0)
        first = bit_of(self.dp, 0) == 0
        return jnp.where(first, block, other), jnp.where(first, other, block)


def body(
    inputs,
    text_state,
    text_segment,
    image_text,
    image_segment,
    self_gain,
    self_shift,
    qkv_weight,
    self_weight,
    cross_gain,
    cross_shift,
    query_weight,
    text_weight,
    cross_weight,
    feed_gain,
    feed_shift,
    up_weight,
    down_weight,
    cotangent,
):
    rows = inputs.shape[0]
    red = Reducer()
    shards = lax.axis_size("seq")
    groups = lax.axis_size("dp")
    me, dp = red.me, red.dp
    per_image = IMG_TOK // rows
    core = bit_of(dp, 0)
    odd = (me % per_image).astype(jnp.int32).reshape(1)
    img_group = image_text.shape[0] // groups
    own_half = core.astype(jnp.int32).reshape(1)
    other_half = 1 - own_half

    def caption_of(group):
        image = group * img_group + me // per_image
        return image_text[image], image_segment[image]

    row, seg = caption_of(dp)
    row_mate, _ = caption_of(dp ^ 1)

    def over_core(block):
        return swap(block, "dp", 0)

    even_to_odd = [(i, i + 1) for i in range(0, shards, 2)]
    odd_to_even = [(i + 1, i) for i in range(0, shards, 2)]
    x_before = lax.ppermute(inputs, "seq", even_to_odd)
    gain1, shift1 = self_gain.reshape(1, D), self_shift.reshape(1, D)
    act1, qkv = norm_project(inputs, gain1, shift1, qkv_weight, 0, "norm_project")
    own_out, own_log = causal_forward(qkv)
    text_row = pick(text_state, row, 0)
    text_row_mate = pick(text_state, row_mate, 0)
    text_kv = jnp.dot(text_row, text_weight, preferred_element_type=F32).astype(BF)
    bias = jnp.where(pick(text_segment, row, 0) == seg, 0.0, NEGATIVE).astype(F32)
    bias = jnp.broadcast_to(bias[:, None], (TEXT_LEN, PAIR))
    act1_before, pairs_before = norm_project(
        x_before, gain1, shift1, qkv_weight, D, "norm_project_before"
    )
    attended, logs = earlier_forward(odd, qkv, pairs_before, own_out, own_log)
    log_rows = logs[:, ::HEAD].T.reshape(HEADS // 2, 2, rows)
    gains = jnp.stack([cross_gain, cross_shift, feed_gain, feed_shift] * 2)
    mid1, act2, cq, crossed, mid2, act3 = middle_forward(
        attended, inputs, self_weight, query_weight, cross_weight, gains, text_kv, bias
    )
    hid_other, dh_other, d_act3 = feed_half(
        other_half, act3, cotangent, up_weight, down_weight, shards, None
    )
    hid_own, dh_own, d_act3 = feed_half(
        own_half, act3, cotangent, up_weight, down_weight, shards, d_act3
    )
    hid_mate, dh_mate = over_core(hid_other), over_core(dh_other)
    cot_mate, act3_mate = over_core(cotangent), over_core(act3)

    top = red.seq_bits - 1
    dp_rest = list(range(1, red.dp_bits))
    seq_all = list(range(red.seq_bits - 1, -1, -1))
    seq_steps = [("seq", b) for b in range(red.seq_bits)]
    dp_steps = [("dp", b) for b in dp_rest]

    def scalars_of(values):
        return jnp.stack([jnp.asarray(v, jnp.int32) for v in values])

    y_bit = dp_rest[0]
    y_mine = bit_of(dp, y_bit)
    col_first = scalars_of([1 - y_mine])
    bw_ff = FF // (2 * shards)
    sent, kept = weight_grad(
        col_first, [hid_own, hid_mate], [cotangent, cot_mate], bw_ff, False, name="down_grad"
    )
    down_sum = add(kept, swap(sent, "dp", y_bit)).reshape([2] * red.seq_bits + [bw_ff, D // 2])
    down_sum = red.finish(down_sum, seq_all, None, dp_steps[1:] + seq_steps)

    def row_first(bit, lefts, rights, width, late=(), name=""):
        sc = scalars_of([0] + red.row_order(bit))
        sent, kept = weight_grad(sc, lefts, rights, width, True, late, name)
        left = [b for b in seq_all if b != bit]
        block = add(kept, swap(sent, "seq", bit))
        return block.reshape([2] * len(left) + [width, block.shape[1]]), left

    bw = D // shards
    up_sum, left = row_first(0, [act3, act3_mate], [dh_own, dh_mate], bw, name="up_grad")
    up_sum = red.finish(up_sum, left, None, seq_steps[1:] + dp_steps)

    g2, dcq, d_mid1, g1, d_att, d_text, d_gains = middle_backward(
        d_act3, mid2, cotangent, mid1, cq, text_kv, bias, cross_weight, query_weight, self_weight, gains
    )

    def core_cols(block):
        wide = block.shape[1] // 2
        return (
            lax.dynamic_slice_in_dim(block, core * wide, wide, 1),
            lax.dynamic_slice_in_dim(block, (1 - core) * wide, wide, 1),
        )

    z_bit = top
    z_first = [("seq", b) for b in range(red.seq_bits) if b != z_bit]

    def square(act, grad, name):
        mine, others = core_cols(grad)
        block, left = row_first(
            z_bit, [act, over_core(act)], [mine, over_core(others)], bw, name=name
        )
        return red.finish(block, left, None, dp_steps + z_first)

    cross_sum = square(crossed, g2, "cross_grad")
    query_sum = square(act2, dcq, "query_grad")
    self_sum = square(attended, g1, "self_grad")
    mine, others = core_cols(d_text)
    block, left = row_first(
        z_bit, [text_row, text_row_mate], [mine, over_core(others)], bw, name="text_weight_grad"
    )
    text_w_sum = red.finish(block, left, None, dp_steps + z_first)

    text_part = jnp.einsum("ke,de->kd", d_text, text_weight, preferred_element_type=F32)
    text_all = jnp.where(
        (jnp.arange(text_state.shape[0]) == row)[:, None, None], text_part[None], 0.0
    ).astype(BF)
    text_flat = text_all.reshape(-1, D)
    text_order = [("dp", b) for b in range(red.dp_bits)] + seq_steps
    for axis, b in text_order:
        mine = bit_of(me if axis == "seq" else dp, b)
        split = text_flat.reshape(2, -1, D)
        text_flat = add(pick(split, mine, 0), swap(pick(split, 1 - mine, 0), axis, b))
    for axis, b in reversed(text_order):
        mine = bit_of(me if axis == "seq" else dp, b) == 0
        other = swap(text_flat, axis, b)
        text_flat = jnp.concatenate(
            [jnp.where(mine, text_flat, other), jnp.where(mine, other, text_flat)], axis=0
        )
    text_grad = text_flat.astype(F32).reshape(text_state.shape)

    sc_other = jnp.concatenate([odd, other_half])
    sc_own = jnp.concatenate([odd, own_half])
    dq_other, dkv_before_other = earlier_backward(
        sc_other, qkv, pairs_before, d_att, attended, log_rows
    )
    dq_own, dkv_before_own = earlier_backward(
        sc_own, qkv, pairs_before, d_att, attended, log_rows
    )
    d_act_before, sums_before = project_back(
        own_half, dkv_before_own, dkv_before_other, qkv_weight, x_before, BF, "project_back_before"
    )
    d_act_late = lax.ppermute(d_act_before, "seq", odd_to_even)
    dqkv_other = causal_backward(sc_other, qkv, d_att, attended, log_rows, dq_other)
    dqkv_own = causal_backward(sc_own, qkv, d_att, attended, log_rows, dq_own)
    d_act, sums_own = project_back(
        own_half, dqkv_own, dqkv_other, qkv_weight, inputs, F32, "project_back"
    )
    block, left = row_first(
        0,
        [act1, over_core(act1), act1_before, over_core(act1_before)],
        [dqkv_own, over_core(dqkv_other), dkv_before_own, over_core(dkv_before_other)],
        bw,
        late=(2, 3),
        name="qkv_grad",
    )
    qkv_sum = red.finish(block, left, None, dp_steps + seq_steps[1:])
    input_grad = input_back(d_act, d_act_late, inputs, d_mid1, gain1)
    output = feed_output(own_half, mid2, hid_own, hid_other, down_weight, shards)

    sums = jnp.concatenate([sums_own[:2] + sums_before[:2], d_gains[:4]], axis=0)
    sums = jnp.concatenate([sums, jnp.zeros((2, D), F32)], axis=0)
    for axis, b in [("dp", b) for b in range(red.dp_bits)] + seq_steps:
        sums = sums + swap(sums, axis, b)
    sums = lax.dynamic_slice_in_dim(sums, me * bw, bw, 1)

    def row_halves(block):
        return red.gather(block, [(b, 0) for b in dp_rest])

    def spread(block):
        first, second = red.both_cores(row_halves(block))
        return jnp.concatenate([first, second], axis=1).astype(F32)

    down_part = red.gather(down_sum, [(y_bit, 1)] + [(b, 0) for b in dp_rest[1:]])
    first, second = red.both_cores(down_part)
    down_grad = jnp.concatenate([first, second], axis=0).astype(F32)
    first, second = red.both_cores(row_halves(up_sum))
    up_grad = (
        jnp.stack([first.reshape(bw, shards, bw_ff), second.reshape(bw, shards, bw_ff)], axis=2)
        .reshape(bw, FF)
        .astype(F32)
    )
    first, second = red.both_cores(row_halves(qkv_sum))
    qkv_grad = (
        jnp.stack([first.reshape(bw, 3, D // 2), second.reshape(bw, 3, D // 2)], axis=2)
        .reshape(bw, 3 * D)
        .astype(F32)
    )
    return (
        output,
        input_grad,
        text_grad,
        sums[0],
        sums[1],
        qkv_grad,
        spread(self_sum),
        sums[2],
        sums[3],
        spread(query_sum),
        spread(text_w_sum),
        spread(cross_sum),
        sums[4],
        sums[5],
        up_grad,
        down_grad,
    )


def solution(mesh):
    tokens = P(("dp", "seq"), None)
    return jax.shard_map(
        body,
        mesh=mesh,
        in_specs=(tokens,) + (P(),) * 17 + (tokens,),
        out_specs=(
            tokens,
            tokens,
            P(),
            P("seq"),
            P("seq"),
            P("seq", None),
            P("seq", None),
            P("seq"),
            P("seq"),
            P("seq", None),
            P("seq", None),
            P("seq", None),
            P("seq"),
            P("seq"),
            P("seq", None),
            P("seq", None),
        ),
        check_vma=False,
    )
```

time: 1020 us -> 645 us (0.63)
  blocking collectives: 272 us -> 0 us
  matrix products: 266 us -> 3.03 us
  Pallas kernels: 0 us -> 214 us
  starting transfers between devices: 13.9 us -> 99 us
  other arithmetic: 82.7 us -> 24.4 us
  waiting for transfers between devices: 308 us -> 261 us
  local copies, waits for them, and re-layouts: 52.5 us -> 27.3 us
  between operations: 16.5 us -> 6.17 us
    dot_general x33 -> x2, matrix products: 247 us -> 3.03 us  [the longest x1 1.52 us: body(): jnp.dot(text_row, text_weight, preferred_element_type=F32).astype(BF)]
    psum x2 -> x0, blocking collectives: 237 us -> none  [the longest x1 231 us: body(): text_total = lax.psum(text_term, ('dp', 'seq'))]
    pallas_call x0 -> x23, Pallas kernels: none -> 214 us  [the longest x7 51.5 us: weight_grad(): pl.pallas_call(kernel, grid_spec=pltpu.PrefetchScalarGridSpec(num_scalar_...]
    reduce_scatter x6 -> x0, waiting for transfers between devices: 184 us -> none  [the longest x1 152 us: body(): lax.psum_scatter(d_up.astype(jnp.bfloat16), 'seq', scatter_dimension=0, t...]
    ppermute x2 -> x74, waiting for transfers between devices: 102 us -> 261 us  [the longest x72 261 us: swap(): return lax.ppermute(block, axis, route)]
    ppermute x2 -> x74, starting transfers between devices: 12.8 us -> 99 us  [the longest x72 92.9 us: swap(): return lax.ppermute(block, axis, route)]
    unnamed x1 -> x0, blocking collectives: 35.1 us -> none
    convert_element_type x15 -> x42, other arithmetic: 44.4 us -> 15.1 us  [the longest x33 6.71 us: add(): return (a.astype(F32) + b.astype(F32)).astype(BF)]
  transfers between devices with their start and end apart: 9 -> 74, of which waited for: 4 -> 36; matrix products, arithmetic and copies ran while one was open for 28% -> 8% of each run, Pallas kernels for 0% -> 22%
where the time goes in v1:
time: 645 us; the launch traced here: 635 us
  waiting for transfers between devices  261 us (40%)
  Pallas kernels  214 us (33%)
  starting transfers between devices  99 us (15%)
  local copies, waits for them, and re-layouts  27.3 us (4%)
  other arithmetic  24.4 us (4%)
    ppermute x72, waiting for transfers between devices, swap(): return lax.ppermute(block, axis, route)  261 us
    ppermute x72, starting transfers between devices, swap(): return lax.ppermute(block, axis, route)  92.9 us
    pallas_call x7, Pallas kernels, weight_grad(): pl.pallas_call(kernel, grid_spec=pltpu.PrefetchScalarGridSpec(num_scalar_...  51.5 us
    pallas_call x2, Pallas kernels, feed_half(): pl.pallas_call(kernel, grid_spec=pltpu.PrefetchScalarGridSpec(num_scalar_...  30.3 us
    pallas_call x2, Pallas kernels, causal_backward(): pl.pallas_call(kernel, grid_spec=pltpu.PrefetchScalarGridSpec(num_scalar_...  20.4 us
    pallas_call x1, Pallas kernels, middle_backward(): pl.pallas_call(kernel, grid=(steps,), in_specs=[row_block, row_block, row...  19.9 us
    pallas_call x2, Pallas kernels, project_back(): pl.pallas_call(kernel, grid_spec=pltpu.PrefetchScalarGridSpec(num_scalar_...  16.5 us
    pallas_call x2, Pallas kernels, norm_project(): pl.pallas_call(kernel, grid=(cols // bn,), in_specs=[whole((rows, width))...  15.8 us
  transfers between devices with their start and end apart: 74, of which 36 were waited for; matrix products, arithmetic and copies ran while one was open for 8% of the time, Pallas kernels for 22%

profile of v1, /device:TPU:0, one launch (start us, length us, event | category | flops | bytes accessed | tf_op | source)
XLA Modules:
  0.0 634.7 jit_solution(16782196618099976341)
XLA Ops:
  18.7 9.1 %norm_project.1 = (bf16[512,1024]{1,0:T(8,128)(2,1)}, bf16[512,3072]{1,0:T(8,128)(2,1)}) custom-call(bf16[512,1024]{1,0:T(8,128)(2,1)} %x_ref.7, f32[1,1024]{1,0:T(1,128)} %bitcast.270, f32[1,1024]{1,0:T(1,128)} %bitcast.273, bf16[1024,3072]{1,0:T(8,128)(2,1)} %wb_ref.3), custom_call_target="tpu_custom_call" | custom-call | flops 3221225472 | bytes 8388608 | tf_op jit(solution)/shard_map/norm_project/pallas_call | solution.py:88
  27.8 13.1 %causal_forward.1 = (f32[512,1024]{1,0:T(8,128)}, f32[512,1024]{1,0:T(8,128)}) custom-call(bf16[512,3072]{1,0:T(8,128)(2,1)} %get-tuple-element.65.q_ref.k_ref.v_ref, bf16[512,3072]{1,0:T(8,128)(2,1)} %get-tuple-element.65.q_ref.k_ref.v_ref, bf16[512,3072]{1,0:T(8,128)(2,1)} %get-tuple-element.65.q_ref.k_ref.v_ref), custom_call_target="tpu_custom_call" | custom-call | flops 2147483648 | bytes 7340032 | tf_op jit(solution)/shard_map/causal_forward/pallas_call | solution.py:132
  43.3 6.8 %norm_project_before.1 = (bf16[512,1024]{1,0:T(8,128)(2,1)}, bf16[512,2048]{1,0:T(8,128)(2,1)}) custom-call(bf16[512,1024]{1,0:T(8,128)(2,1)} %copy-done.10, f32[1,1024]{1,0:T(1,128)} %bitcast.271, f32[1,1024]{1,0:T(1,128)} %bitcast.274, bf16[1024,3072]{1,0:T(8,128)(2,1)} %wb_ref.3), custom_call_target="tpu_custom_call" | custom-call | flops 2147483648 | bytes 6291456 | tf_op jit(solution)/shard_map/norm_project_before/pallas_call | solution.py:88
  50.1 7.2 %earlier_forward.1 = (bf16[512,1024]{1,0:T(8,128)(2,1)}, f32[512,1024]{1,0:T(8,128)}) custom-call(s32[1]{0:T(128)} %bitcast.1.odd_ref, bf16[512,3072]{1,0:T(8,128)(2,1)} %get-tuple-element.65.q_ref.k_ref.v_ref, bf16[512,2048]{1,0:T(8,128)(2,1)} %get-tuple-element.66.k_ref.v_ref, bf16[512,2048]{1,0:T(8,128)(2,1)} %get-tuple-element.66.k_ref.v_ref, ...), custom_call_target="tpu_custom_call" | custom-call | flops 2147483648 | bytes 9437184 | tf_op jit(solution)/shard_map/earlier_forward/pallas_call | solution.py:185
  58.0 11.6 %middle_forward.1 = (f32[512,1024]{1,0:T(8,128)}, bf16[512,1024]{1,0:T(8,128)(2,1)}, bf16[512,1024]{1,0:T(8,128)(2,1)}, bf16[512,1024]{1,0:T(8,128)(2,1)}, f32[5...) custom-call(bf16[512,1024]{1,0:T(8,128)(2,1)} %get-tuple-element.69.at_ref.out_ref.refs_0_, bf16[512,1024]{1,0:T(8,128)(2,1)} %x_ref.7, ...), custom_call_target="tpu_custom_call" | custom-call | flops 4294967296 | bytes 16777216 | tf_op jit(solution)/shard_map/middle_forward/pallas_call | solution.py:238
  69.6 14.7 %feed_half.2 = (bf16[512,2048]{1,0:T(8,128)(2,1)}, bf16[512,2048]{1,0:T(8,128)(2,1)}, f32[512,1024]{1,0:T(8,128)}) custom-call(s32[1]{0:T(128)S(6)} %sub.18.which_ref, bf16[512,1024]{1,0:T(8,128)(2,1)} %get-tuple-element.71.a_ref.refs_0_, bf16[512,1024]{1,0:T(8,128)(2,1)} %refs_4_.1, bf16[1024,4096]{1,0:T(8,128)(2,1)} %up_ref.3, bf16[4096,1024]{1,0:T(8,128)(2,1)} %db_ref.1), custom_call_target="tpu_custom_call" | custom-call | flops 6442450944 | bytes 12582912 | tf_op jit(solution)/shard_map/feed_half/pallas_call | solution.py:297
  84.3 15.5 %feed_half.3 = (bf16[512,2048]{1,0:T(8,128)(2,1)}, bf16[512,2048]{1,0:T(8,128)(2,1)}, f32[512,1024]{1,0:T(8,128)}) custom-call(s32[1]{0:T(128)} %bitcast.which_ref.own_ref, bf16[512,1024]{1,0:T(8,128)(2,1)} %get-tuple-element.71.a_ref.refs_0_, bf16[512,1024]{1,0:T(8,128)(2,1)} %refs_4_.1, bf16[1024,4096]{1,0:T(8,128)(2,1)} %up_ref.3, ...), custom_call_target="tpu_custom_call" | custom-call | flops 6442450944 | bytes 12582912 | tf_op jit(solution)/shard_map/feed_half/pallas_call | solution.py:297
  99.9 19.9 %middle_backward.1 = (bf16[512,1024]{1,0:T(8,128)(2,1)}, bf16[512,1024]{1,0:T(8,128)(2,1)}, f32[512,1024]{1,0:T(8,128)}, bf16[512,1024]{1,0:T(8,128)(2,1)}, bf16...) custom-call(f32[512,1024]{1,0:T(8,128)} %get-tuple-element.75.da3_ref, ...), custom_call_target="tpu_custom_call" | custom-call | flops 5368709120 | bytes 18874368 | tf_op jit(solution)/shard_map/middle_backward/pallas_call | solution.py:422
  131.1 10.1 %causal_backward.3.gb_ref = bf16[3,512,512]{2,1,0:T(8,128)(2,1)} custom-call(s32[2]{0:T(128)} %pad_add_fusion.1.sc_ref, bf16[512,3072]{1,0:T(8,128)(2,1)} %get-tuple-element.65.q_ref.k_ref.v_ref, bf16[512,3072]{1,0:T(8,128)(2,1)} %get-tuple-element.65.q_ref.k_ref.v_ref, bf16[512,3072]{1,0:T(8,128)(2,1)} %get-tuple-element.65.q_ref.k_ref.v_ref, ...), custom_call_target="tpu_custom_call" | custom-call | flops 2684354560 | bytes 7340032 | tf_op jit(solution)/shard_map/causal_backward/pallas_call | solution.py:567
  146.5 10.3 %causal_backward.2.ga_ref.refs_4_ = bf16[3,512,512]{2,1,0:T(8,128)(2,1)} custom-call(s32[2]{0:T(128)} %pad_add_fusion.sc_ref, bf16[512,3072]{1,0:T(8,128)(2,1)} %get-tuple-element.65.q_ref.k_ref.v_ref, bf16[512,3072]{1,0:T(8,128)(2,1)} %get-tuple-element.65.q_ref.k_ref.v_ref, bf16[512,3072]{1,0:T(8,128)(2,1)} %get-tuple-element.65.q_ref.k_ref.v_ref, ...), custom_call_target="tpu_custom_call" | custom-call | flops 2684354560 | bytes 7340032 | tf_op jit(solution)/shard_map/causal_backward/pallas_call | solution.py:567
  156.7 9.3 %project_back.1 = (f32[512,1024]{1,0:T(8,128)}, f32[8,1024]{1,0:T(8,128)}) custom-call(s32[1]{0:T(128)} %bitcast.which_ref.own_ref, bf16[3,512,512]{2,1,0:T(8,128)(2,1)} %causal_backward.2.ga_ref.refs_4_, bf16[3,512,512]{2,1,0:T(8,128)(2,1)} %causal_backward.3.gb_ref, bf16[1024,3072]{1,0:T(8,128)(2,1)} %wb_ref.3, bf16[1024,3072]{1,0:T(8,128)(2,1)} %wb_ref.3, ...), custom_call_target="tpu_custom_call" | custom-call | flops 3221225472 | bytes 10485760 | tf_op jit(solution)/shard_map/project_back/pallas_call | solution.py:617
  166.0 7.2 %project_back_before.1 = (bf16[512,1024]{1,0:T(8,128)(2,1)}, f32[8,1024]{1,0:T(8,128)}) custom-call(s32[1]{0:T(128)} %bitcast.which_ref.own_ref, bf16[2,512,512]{2,1,0:T(8,128)(2,1)} %get-tuple-element.83.ga_ref.refs_6_, bf16[2,512,512]{2,1,0:T(8,128)(2,1)} %get-tuple-element.84.gb_ref, bf16[1024,3072]{1,0:T(8,128)(2,1)} %wb_ref.3, ...), custom_call_target="tpu_custom_call" | custom-call | flops 2147483648 | bytes 8388608 | tf_op jit(solution)/shard_map/project_back_before/pallas_call | solution.py:617
  179.7 19.9 %collective-permute-start.14 = (f32[8,1024]{1,0:T(8,128)S(1)}, f32[8,1024]{1,0:T(8,128)S(1)}, u32[]{:S(2)}, u32[]{:S(2)}) collective-permute-start(f32[8,1024]{1,0:T(8,128)S(1)} %add.339), channel_id=1, source_target_pairs={{0,1},{1,0},{2,3},{3,2},{4,5},{5,4},{6,7},{7,6},{8,9},{9,8},{10,11... | collective-permute-start | bytes 98312 | tf_op jit(solution)/shard_map/ppermute | solution.py:763
  213.3 12.6 %feed_output.1 = bf16[512,1024]{1,0:T(8,128)(2,1)} custom-call(s32[1]{0:T(128)} %bitcast.which_ref.own_ref, f32[512,1024]{1,0:T(8,128)} %get-tuple-element.70.mid_ref.mid2_ref, bf16[512,2048]{1,0:T(8,128)(2,1)} %get-tuple-element.73.a_ref.refs_0_, bf16[512,2048]{1,0:T(8,128)(2,1)} %get-tuple-element.74.b_ref, bf16[4096,1024]{1,0:T(8,128)(2,1)} %db_ref.1, ...), custom_call_target="tpu_custom_call" | custom-call | flops 4294967296 | bytes 15728640 | tf_op jit(solution)/shard_map/feed_output/pallas_call | solution.py:338
  262.0 40.5 %collective-permute-done.44 = bf16[512,1024]{1,0:T(8,128)(2,1)S(1)} collective-permute-done((bf16[512,1024]{1,0:T(8,128)(2,1)}, bf16[512,1024]{1,0:T(8,128)(2,1)S(1)}, u32[]{:S(2)}, u32[]{:S(2)}) %collective-permute-start.44) | collective-permute-done | bytes 1048608 | tf_op jit(solution)/shard_map/ppermute | solution.py:763
  303.0 10.8 %collective-permute-done.37 = bf16[512,512]{1,0:T(8,128)(2,1)S(1)} collective-permute-done((bf16[512,512]{1,0:T(8,128)(2,1)}, bf16[512,512]{1,0:T(8,128)(2,1)S(1)}, u32[]{:S(2)}, u32[]{:S(2)}) %collective-permute-start.37) | collective-permute-done | bytes 524320 | tf_op jit(solution)/shard_map/ppermute | solution.py:763
  314.0 10.6 %collective-permute-done.52 = bf16[512,512]{1,0:T(8,128)(2,1)S(1)} collective-permute-done((bf16[512,512]{1,0:T(8,128)(2,1)}, bf16[512,512]{1,0:T(8,128)(2,1)S(1)}, u32[]{:S(2)}, u32[]{:S(2)}) %collective-permute-start.52) | collective-permute-done | bytes 524320 | tf_op jit(solution)/shard_map/ppermute | solution.py:763
  325.7 24.4 %collective-permute-done.29 = bf16[512,512]{1,0:T(8,128)(2,1)S(1)} collective-permute-done((bf16[512,512]{1,0:T(8,128)(2,1)S(1)}, bf16[512,512]{1,0:T(8,128)(2,1)S(1)}, u32[]{:S(2)}, u32[]{:S(2)}) %collective-permute-start.29) | collective-permute-done | bytes 524320 | tf_op jit(solution)/shard_map/ppermute | solution.py:763
  353.8 13.1 %qkv_grad.1 = (bf16[512,1536]{1,0:T(8,128)(2,1)}, bf16[512,1536]{1,0:T(8,128)(2,1)}) custom-call(s32[9]{0:T(128)} %stack.65.sc_ref, bf16[512,1024]{1,0:T(8,128)(2,1)} %get-tuple-element.91.refs_0_, bf16[512,1024]{1,0:T(8,128)(2,1)} %collective-permute-done.17.refs_1_, bf16[512,1024]{1,0:T(8,128)(2,1)} %get-tuple-element.92.refs_2_, ...), custom_call_target="tpu_custom_call" | custom-call | flops 6442450944 | bytes 13631488 | tf_op jit(solution)/shard_map/qkv_grad/pallas_call | solution.py:743
  378.8 14.7 %collective-permute-done.30 = bf16[2,2,64,512]{3,2,0,1:T(8,128)(2,1)S(1)} collective-permute-done((bf16[2,2,64,512]{3,2,0,1:T(8,128)(2,1)S(1)}, bf16[2,2,64,512]{3,2,0,1:T(8,128)(2,1)S(1)}, u32[]{:S(2)}, u32[]{:S(2)}) %collective-permute-start.30) | collective-permute-done | bytes 262176 | tf_op jit(solution)/shard_map/ppermute | solution.py:763
  396.7 6.8 %collective-permute-done.4 = bf16[128,1024]{1,0:T(8,128)(2,1)S(1)} collective-permute-done((bf16[128,1024]{1,0:T(8,128)(2,1)S(1)}, bf16[128,1024]{1,0:T(8,128)(2,1)S(1)}, u32[]{:S(2)}, u32[]{:S(2)}) %collective-permute-start.4) | collective-permute-done | bytes 262176 | tf_op jit(solution)/shard_map/ppermute | solution.py:763
  437.9 8.8 %down_grad.1 = (bf16[2048,512]{1,0:T(8,128)(2,1)}, bf16[2048,512]{1,0:T(8,128)(2,1)}) custom-call(s32[1]{0:T(128)} %bitcast.102.sc_ref, bf16[512,2048]{1,0:T(8,128)(2,1)} %get-tuple-element.73.a_ref.refs_0_, bf16[512,2048]{1,0:T(8,128)(2,1)} %collective-permute-done.66.refs_1_, bf16[512,1024]{1,0:T(8,128)(2,1)} %refs_4_.1, ...), custom_call_target="tpu_custom_call" | custom-call | flops 4294967296 | bytes 10485760 | tf_op jit(solution)/shard_map/down_grad/pallas_call | solution.py:743
  448.3 9.7 %up_grad.1 = (bf16[512,2048]{1,0:T(8,128)(2,1)}, bf16[512,2048]{1,0:T(8,128)(2,1)}) custom-call(s32[9]{0:T(128)} %stack.65.sc_ref, bf16[512,1024]{1,0:T(8,128)(2,1)} %get-tuple-element.71.a_ref.refs_0_, bf16[512,1024]{1,0:T(8,128)(2,1)} %copy-done.25, bf16[512,2048]{1,0:T(8,128)(2,1)} %get-tuple-element.108.refs_2_, ...), custom_call_target="tpu_custom_call" | custom-call | flops 4294967296 | bytes 10485760 | tf_op jit(solution)/shard_map/up_grad/pallas_call | solution.py:743
  476.2 26.1 %collective-permute-done.48 = bf16[64,1024]{1,0:T(8,128)(2,1)S(1)} collective-permute-done((bf16[64,1024]{1,0:T(8,128)(2,1)S(1)}, bf16[64,1024]{1,0:T(8,128)(2,1)S(1)}, u32[]{:S(2)}, u32[]{:S(2)}) %collective-permute-start.48) | collective-permute-done | bytes 131104 | tf_op jit(solution)/shard_map/ppermute | solution.py:763
  502.4 13.2 %collective-permute-done.9 = bf16[128,1024]{1,0:T(8,128)(2,1)S(1)} collective-permute-done((bf16[128,1024]{1,0:T(8,128)(2,1)S(1)}, bf16[128,1024]{1,0:T(8,128)(2,1)S(1)}, u32[]{:S(2)}, u32[]{:S(2)}) %collective-permute-start.9) | collective-permute-done | bytes 262176 | tf_op jit(solution)/shard_map/ppermute | solution.py:763
  518.4 12.3 %collective-permute-done.10 = bf16[256,1024]{1,0:T(8,128)(2,1)S(1)} collective-permute-done((bf16[256,1024]{1,0:T(8,128)(2,1)S(1)}, bf16[256,1024]{1,0:T(8,128)(2,1)S(1)}, u32[]{:S(2)}, u32[]{:S(2)}) %collective-permute-start.10) | collective-permute-done | bytes 524320 | tf_op jit(solution)/shard_map/ppermute | solution.py:763
  532.3 8.1 %collective-permute-done.22 = bf16[2,2,64,1536]{3,2,1,0:T(8,128)(2,1)S(1)} collective-permute-done((bf16[2,2,64,1536]{3,2,1,0:T(8,128)(2,1)S(1)}, bf16[2,2,64,1536]{3,2,1,0:T(8,128)(2,1)S(1)}, u32[]{:S(2)}, u32[]{:S(2)}) %collective-permute-start.22) | collective-permute-done | bytes 786464 | tf_op jit(solution)/shard_map/ppermute | solution.py:763
  548.9 7.6 %collective-permute-start.24 = (bf16[64,1536]{1,0:T(8,128)(2,1)S(1)}, bf16[64,1536]{1,0:T(8,128)(2,1)S(1)}, u32[]{:S(2)}, u32[]{:S(2)}) collective-permute-start(bf16[64,1536]{1,0:T(8,128)(2,1)S(1)} %dynamic-slice_bitcast_fusion.13), channel_id=1, source_target_pairs={{0,4},{1,5},{2,6},{3,7},{4,0},{5,1},{6,2},{7,3},{8,12},{9,13},{10,... | collective-permute-start | bytes 589832 | tf_op jit(solution)/shard_map/ppermute | solution.py:763
  568.0 8.6 %collective-permute-done.61 = bf16[2,128,2048]{2,1,0:T(8,128)(2,1)S(1)} collective-permute-done((bf16[2,128,2048]{2,1,0:T(8,128)(2,1)S(1)}, bf16[2,128,2048]{2,1,0:T(8,128)(2,1)S(1)}, u32[]{:S(2)}, u32[]{:S(2)}) %collective-permute-start.61) | collective-permute-done | bytes 1048608 | tf_op jit(solution)/shard_map/ppermute | solution.py:763
  577.1 6.9 %collective-permute-start.62 = (bf16[128,2048]{1,0:T(8,128)(2,1)S(1)}, bf16[128,2048]{1,0:T(8,128)(2,1)S(1)}, u32[]{:S(2)}, u32[]{:S(2)}) collective-permute-start(bf16[128,2048]{1,0:T(8,128)(2,1)S(1)} %dynamic-slice_bitcast_fusion.4), channel_id=1, source_target_pairs={{0,4},{1,5},{2,6},{3,7},{4,0},{5,1},{6,2},{7,3},{8,12},{9,13},{10,... | collective-permute-start | bytes 1572872 | tf_op jit(solution)/shard_map/ppermute | solution.py:763
  584.6 12.5 %collective-permute-done.62 = bf16[128,2048]{1,0:T(8,128)(2,1)S(1)} collective-permute-done((bf16[128,2048]{1,0:T(8,128)(2,1)S(1)}, bf16[128,2048]{1,0:T(8,128)(2,1)S(1)}, u32[]{:S(2)}, u32[]{:S(2)}) %collective-permute-start.62) | collective-permute-done | bytes 524320 | tf_op jit(solution)/shard_map/ppermute | solution.py:763
  607.9 11.3 %collective-permute-done.71 = bf16[256,512]{1,0:T(8,128)(2,1)S(1)} collective-permute-done((bf16[256,512]{1,0:T(8,128)(2,1)S(1)}, bf16[256,512]{1,0:T(8,128)(2,1)S(1)}, u32[]{:S(2)}, u32[]{:S(2)}) %collective-permute-start.71) | collective-permute-done | bytes 262176 | tf_op jit(solution)/shard_map/ppermute | solution.py:763
  (338 shorter events, 215.4 us)
Async XLA Ops:
  0.6 41.7 %collective-permute-start = (bf16[512,1024]{1,0:T(8,128)(2,1)}, bf16[512,1024]{1,0:T(8,128)(2,1)S(1)}, u32[]{:S(2)}, u32[]{:S(2)}) collective-permute-start(bf16[512,1024]{1,0:T(8,128)(2,1)} %x_ref.7), channel_id=1, source_target_pairs={{0,1},{2,3},{4,5},{6,7},{8,9},{10,11},{12,13},{14,15},{16,17},{18,... | collective-permute-start | bytes 3145736 | tf_op jit(solution)/shard_map/ppermute | solution.py:872
  121.8 90.2 %collective-permute-start.36 = (bf16[512,512]{1,0:T(8,128)(2,1)S(1)}, bf16[512,512]{1,0:T(8,128)(2,1)}, u32[]{:S(2)}, u32[]{:S(2)}) collective-permute-start(bf16[512,512]{1,0:T(8,128)(2,1)S(1)} %get-tuple-element.178), channel_id=1, source_target_pairs={{0,8},{8,0},{16,24},{24,16},{1,9},{9,1},{17,25},{25,17},{2,10},{10... | collective-permute-start | bytes 1572872 | tf_op jit(solution)/shard_map/ppermute | solution.py:763
  121.9 108.6 %collective-permute-start.35 = (bf16[512,1024]{1,0:T(8,128)(2,1)}, bf16[512,1024]{1,0:T(8,128)(2,1)}, u32[]{:S(2)}, u32[]{:S(2)}) collective-permute-start(bf16[512,1024]{1,0:T(8,128)(2,1)} %get-tuple-element.98.refs_0_), channel_id=1, source_target_pairs={{0,8},{8,0},{16,24},{24,16},{1,9},{9,1},{17,25},{25,17},{2,10},{10... | collective-permute-start | bytes 3145736 | tf_op jit(solution)/shard_map/ppermute | solution.py:763
  178.0 33.5 %collective-permute-start.43 = (bf16[128,1024]{1,0:T(8,128)(2,1)S(1)}, bf16[128,1024]{1,0:T(8,128)(2,1)}, u32[]{:S(2)}, u32[]{:S(2)}) collective-permute-start(bf16[128,1024]{1,0:T(8,128)(2,1)S(1)} %get-tuple-element.194), channel_id=1, source_target_pairs={{0,8},{8,0},{16,24},{24,16},{1,9},{9,1},{17,25},{25,17},{2,10},{10... | collective-permute-start | bytes 786440 | tf_op jit(solution)/shard_map/ppermute | solution.py:763
  179.7 21.8 %collective-permute-start.14 = (f32[8,1024]{1,0:T(8,128)S(1)}, f32[8,1024]{1,0:T(8,128)S(1)}, u32[]{:S(2)}, u32[]{:S(2)}) collective-permute-start(f32[8,1024]{1,0:T(8,128)S(1)} %add.339), channel_id=1, source_target_pairs={{0,1},{1,0},{2,3},{3,2},{4,5},{5,4},{6,7},{7,6},{8,9},{9,8},{10,11... | collective-permute-start | bytes 98312 | tf_op jit(solution)/shard_map/ppermute | solution.py:763
  204.2 30.6 %collective-permute-start.2 = (bf16[512,1024]{1,0:T(8,128)(2,1)}, bf16[512,1024]{1,0:T(8,128)(2,1)}, u32[]{:S(2)}, u32[]{:S(2)}) collective-permute-start(bf16[512,1024]{1,0:T(8,128)(2,1)} %dynamic-slice_bitcast_fusion.1), channel_id=1, source_target_pairs={{0,8},{8,0},{16,24},{24,16},{1,9},{9,1},{17,25},{25,17},{2,10},{10... | collective-permute-start | bytes 3145736 | tf_op jit(solution)/shard_map/ppermute | solution.py:763
  211.5 36.9 %collective-permute-start.50 = (bf16[512,1024]{1,0:T(8,128)(2,1)}, bf16[512,1024]{1,0:T(8,128)(2,1)}, u32[]{:S(2)}, u32[]{:S(2)}) collective-permute-start(bf16[512,1024]{1,0:T(8,128)(2,1)} %get-tuple-element.104.refs_0_), channel_id=1, source_target_pairs={{0,8},{8,0},{16,24},{24,16},{1,9},{9,1},{17,25},{25,17},{2,10},{10... | collective-permute-start | bytes 3145736 | tf_op jit(solution)/shard_map/ppermute | solution.py:763
  212.0 29.7 %collective-permute-start.1 = (bf16[512,1024]{1,0:T(8,128)(2,1)}, bf16[512,1024]{1,0:T(8,128)(2,1)S(1)}, u32[]{:S(2)}, u32[]{:S(2)}) collective-permute-start(bf16[512,1024]{1,0:T(8,128)(2,1)} %get-tuple-element.85), channel_id=1, source_target_pairs={{1,0},{3,2},{5,4},{7,6},{9,8},{11,10},{13,12},{15,14},{17,16},{19,... | collective-permute-start | bytes 3145736 | tf_op jit(solution)/shard_map/ppermute | solution.py:988
  230.4 23.9 %collective-permute-start.27 = (bf16[512,1024]{1,0:T(8,128)(2,1)S(1)}, bf16[512,1024]{1,0:T(8,128)(2,1)}, u32[]{:S(2)}, u32[]{:S(2)}) collective-permute-start(bf16[512,1024]{1,0:T(8,128)(2,1)S(1)} %copy-done.3), channel_id=1, source_target_pairs={{0,8},{8,0},{16,24},{24,16},{1,9},{9,1},{17,25},{25,17},{2,10},{10... | collective-permute-start | bytes 3145736 | tf_op jit(solution)/shard_map/ppermute | solution.py:763
  230.5 72.1 %collective-permute-start.44 = (bf16[512,1024]{1,0:T(8,128)(2,1)}, bf16[512,1024]{1,0:T(8,128)(2,1)S(1)}, u32[]{:S(2)}, u32[]{:S(2)}) collective-permute-start(bf16[512,1024]{1,0:T(8,128)(2,1)} %get-tuple-element.103), channel_id=1, source_target_pairs={{0,4},{1,5},{2,6},{3,7},{4,0},{5,1},{6,2},{7,3},{8,12},{9,13},{10,... | collective-permute-start | bytes 3145736 | tf_op jit(solution)/shard_map/ppermute | solution.py:763
  241.8 72.0 %collective-permute-start.37 = (bf16[512,512]{1,0:T(8,128)(2,1)}, bf16[512,512]{1,0:T(8,128)(2,1)S(1)}, u32[]{:S(2)}, u32[]{:S(2)}) collective-permute-start(bf16[512,512]{1,0:T(8,128)(2,1)} %get-tuple-element.101), channel_id=1, source_target_pairs={{0,4},{1,5},{2,6},{3,7},{4,0},{5,1},{6,2},{7,3},{8,12},{9,13},{10,... | collective-permute-start | bytes 1572872 | tf_op jit(solution)/shard_map/ppermute | solution.py:763
  248.4 104.1 %collective-permute-start.19 = (bf16[3,512,512]{2,1,0:T(8,128)(2,1)S(1)}, bf16[3,512,512]{2,1,0:T(8,128)(2,1)}, u32[]{:S(2)}, u32[]{:S(2)}) collective-permute-start(bf16[3,512,512]{2,1,0:T(8,128)(2,1)S(1)} %copy-done.2), channel_id=1, source_target_pairs={{0,8},{8,0},{16,24},{24,16},{1,9},{9,1},{17,25},{25,17},{2,10},{10... | collective-permute-start | bytes 4718600 | tf_op jit(solution)/shard_map/ppermute | solution.py:763
  253.9 96.4 %collective-permute-start.17 = (bf16[512,1024]{1,0:T(8,128)(2,1)}, bf16[512,1024]{1,0:T(8,128)(2,1)}, u32[]{:S(2)}, u32[]{:S(2)}) collective-permute-start(bf16[512,1024]{1,0:T(8,128)(2,1)} %get-tuple-element.91.refs_0_), channel_id=1, source_target_pairs={{0,8},{8,0},{16,24},{24,16},{1,9},{9,1},{17,25},{25,17},{2,10},{10... | collective-permute-start | bytes 3145736 | tf_op jit(solution)/shard_map/ppermute | solution.py:763
  254.2 70.3 %collective-permute-start.52 = (bf16[512,512]{1,0:T(8,128)(2,1)}, bf16[512,512]{1,0:T(8,128)(2,1)S(1)}, u32[]{:S(2)}, u32[]{:S(2)}) collective-permute-start(bf16[512,512]{1,0:T(8,128)(2,1)} %get-tuple-element.107), channel_id=1, source_target_pairs={{0,4},{1,5},{2,6},{3,7},{4,0},{5,1},{6,2},{7,3},{8,12},{9,13},{10,... | collective-permute-start | bytes 1572872 | tf_op jit(solution)/shard_map/ppermute | solution.py:763
  302.6 48.4 %collective-permute-start.20 = (bf16[2,512,512]{2,1,0:T(8,128)(2,1)S(1)}, bf16[2,512,512]{2,1,0:T(8,128)(2,1)S(1)}, u32[]{:S(2)}, u32[]{:S(2)}) collective-permute-start(bf16[2,512,512]{2,1,0:T(8,128)(2,1)S(1)} %copy-done.9), channel_id=1, source_target_pairs={{0,8},{8,0},{16,24},{24,16},{1,9},{9,1},{17,25},{25,17},{2,10},{10... | collective-permute-start | bytes 3145736 | tf_op jit(solution)/shard_map/ppermute | solution.py:763
  313.8 37.2 %collective-permute-start.18 = (bf16[512,1024]{1,0:T(8,128)(2,1)S(1)}, bf16[512,1024]{1,0:T(8,128)(2,1)S(1)}, u32[]{:S(2)}, u32[]{:S(2)}) collective-permute-start(bf16[512,1024]{1,0:T(8,128)(2,1)S(1)} %copy-done.22), channel_id=1, source_target_pairs={{0,8},{8,0},{16,24},{24,16},{1,9},{9,1},{17,25},{25,17},{2,10},{10... | collective-permute-start | bytes 3145736 | tf_op jit(solution)/shard_map/ppermute | solution.py:763
  324.6 25.6 %collective-permute-start.29 = (bf16[512,512]{1,0:T(8,128)(2,1)S(1)}, bf16[512,512]{1,0:T(8,128)(2,1)S(1)}, u32[]{:S(2)}, u32[]{:S(2)}) collective-permute-start(bf16[512,512]{1,0:T(8,128)(2,1)S(1)} %copy-done.26), channel_id=1, source_target_pairs={{0,4},{1,5},{2,6},{3,7},{4,0},{5,1},{6,2},{7,3},{8,12},{9,13},{10,... | collective-permute-start | bytes 1572872 | tf_op jit(solution)/shard_map/ppermute | solution.py:763
  350.2 85.6 %collective-permute-start.67 = (bf16[512,1024]{1,0:T(8,128)(2,1)}, bf16[512,1024]{1,0:T(8,128)(2,1)}, u32[]{:S(2)}, u32[]{:S(2)}) collective-permute-start(bf16[512,1024]{1,0:T(8,128)(2,1)} %refs_4_.1), channel_id=1, source_target_pairs={{0,8},{8,0},{16,24},{24,16},{1,9},{9,1},{17,25},{25,17},{2,10},{10... | collective-permute-start | bytes 3145736 | tf_op jit(solution)/shard_map/ppermute | solution.py:763
  350.3 87.0 %collective-permute-start.66 = (bf16[512,2048]{1,0:T(8,128)(2,1)S(1)}, bf16[512,2048]{1,0:T(8,128)(2,1)}, u32[]{:S(2)}, u32[]{:S(2)}) collective-permute-start(bf16[512,2048]{1,0:T(8,128)(2,1)S(1)} %copy-done.7), channel_id=1, source_target_pairs={{0,8},{8,0},{16,24},{24,16},{1,9},{9,1},{17,25},{25,17},{2,10},{10... | collective-permute-start | bytes 6291464 | tf_op jit(solution)/shard_map/ppermute | solution.py:763
  350.9 97.3 %collective-permute-start.59 = (bf16[512,2048]{1,0:T(8,128)(2,1)}, bf16[512,2048]{1,0:T(8,128)(2,1)}, u32[]{:S(2)}, u32[]{:S(2)}) collective-permute-start(bf16[512,2048]{1,0:T(8,128)(2,1)} %get-tuple-element.109), channel_id=1, source_target_pairs={{0,8},{8,0},{16,24},{24,16},{1,9},{9,1},{17,25},{25,17},{2,10},{10... | collective-permute-start | bytes 6291464 | tf_op jit(solution)/shard_map/ppermute | solution.py:763
  371.6 24.8 %collective-permute-start.45 = (bf16[2,2,64,1024]{3,2,0,1:T(8,128)(2,1)S(1)}, bf16[2,2,64,1024]{3,2,0,1:T(8,128)(2,1)S(1)}, u32[]{:S(2)}, u32[]{:S(2)}) collective-permute-start(bf16[2,2,64,1024]{3,2,0,1:T(8,128)(2,1)S(1)} %bitcast.258), channel_id=1, source_target_pairs={{0,16},{8,24},{16,0},{24,8},{1,17},{9,25},{17,1},{25,9},{2,18},{10... | collective-permute-start | bytes 1572872 | tf_op jit(solution)/shard_map/ppermute | solution.py:763
  420.8 25.9 %collective-permute-start.58 = (bf16[512,1024]{1,0:T(8,128)(2,1)S(1)}, bf16[512,1024]{1,0:T(8,128)(2,1)S(1)}, u32[]{:S(2)}, u32[]{:S(2)}) collective-permute-start(bf16[512,1024]{1,0:T(8,128)(2,1)S(1)} %copy-done.21), channel_id=1, source_target_pairs={{0,8},{8,0},{16,24},{24,16},{1,9},{9,1},{17,25},{25,17},{2,10},{10... | collective-permute-start | bytes 3145736 | tf_op jit(solution)/shard_map/ppermute | solution.py:763
  433.3 84.0 %collective-permute-start.21 = (bf16[512,1536]{1,0:T(8,128)(2,1)}, bf16[512,1536]{1,0:T(8,128)(2,1)S(1)}, u32[]{:S(2)}, u32[]{:S(2)}) collective-permute-start(bf16[512,1536]{1,0:T(8,128)(2,1)} %get-tuple-element.94), channel_id=1, source_target_pairs={{0,1},{1,0},{2,3},{3,2},{4,5},{5,4},{6,7},{7,6},{8,9},{9,8},{10,11... | collective-permute-start | bytes 4718600 | tf_op jit(solution)/shard_map/ppermute | solution.py:763
  435.8 22.2 %collective-permute-start.56 = (bf16[64,512]{1,0:T(8,128)(2,1)S(1)}, bf16[64,512]{1,0:T(8,128)(2,1)S(1)}, u32[]{:S(2)}, u32[]{:S(2)}) collective-permute-start(bf16[64,512]{1,0:T(8,128)(2,1)S(1)} %fusion.23), channel_id=1, source_target_pairs={{0,16},{8,24},{16,0},{24,8},{1,17},{9,25},{17,1},{25,9},{2,18},{10... | collective-permute-start | bytes 196616 | tf_op jit(solution)/shard_map/ppermute | solution.py:763
  437.4 21.6 %collective-permute-start.41 = (bf16[64,512]{1,0:T(8,128)(2,1)S(1)}, bf16[64,512]{1,0:T(8,128)(2,1)S(1)}, u32[]{:S(2)}, u32[]{:S(2)}) collective-permute-start(bf16[64,512]{1,0:T(8,128)(2,1)S(1)} %fusion.24), channel_id=1, source_target_pairs={{0,16},{8,24},{16,0},{24,8},{1,17},{9,25},{17,1},{25,9},{2,18},{10... | collective-permute-start | bytes 196616 | tf_op jit(solution)/shard_map/ppermute | solution.py:763
  458.0 105.9 %collective-permute-start.68 = (bf16[2048,512]{1,0:T(8,128)(2,1)S(1)}, bf16[2048,512]{1,0:T(8,128)(2,1)S(1)}, u32[]{:S(2)}, u32[]{:S(2)}) collective-permute-start(bf16[2048,512]{1,0:T(8,128)(2,1)S(1)} %copy-done.20), channel_id=1, source_target_pairs={{0,16},{8,24},{16,0},{24,8},{1,17},{9,25},{17,1},{25,9},{2,18},{10... | collective-permute-start | bytes 6291464 | tf_op jit(solution)/shard_map/ppermute | solution.py:763
  459.0 86.7 %collective-permute-start.60 = (bf16[512,2048]{1,0:T(8,128)(2,1)}, bf16[512,2048]{1,0:T(8,128)(2,1)S(1)}, u32[]{:S(2)}, u32[]{:S(2)}) collective-permute-start(bf16[512,2048]{1,0:T(8,128)(2,1)} %get-tuple-element.111), channel_id=1, source_target_pairs={{0,1},{1,0},{2,3},{3,2},{4,5},{5,4},{6,7},{7,6},{8,9},{9,8},{10,11... | collective-permute-start | bytes 6291464 | tf_op jit(solution)/shard_map/ppermute | solution.py:763
  470.0 32.3 %collective-permute-start.48 = (bf16[64,1024]{1,0:T(8,128)(2,1)S(1)}, bf16[64,1024]{1,0:T(8,128)(2,1)S(1)}, u32[]{:S(2)}, u32[]{:S(2)}) collective-permute-start(bf16[64,1024]{1,0:T(8,128)(2,1)S(1)} %fusion.19), channel_id=1, source_target_pairs={{0,16},{8,24},{16,0},{24,8},{1,17},{9,25},{17,1},{25,9},{2,18},{10... | collective-permute-start | bytes 393224 | tf_op jit(solution)/shard_map/ppermute | solution.py:763
  472.4 43.2 %collective-permute-start.9 = (bf16[128,1024]{1,0:T(8,128)(2,1)S(1)}, bf16[128,1024]{1,0:T(8,128)(2,1)S(1)}, u32[]{:S(2)}, u32[]{:S(2)}) collective-permute-start(bf16[128,1024]{1,0:T(8,128)(2,1)S(1)} %pad_maximum_fusion.6), channel_id=1, source_target_pairs={{0,1},{1,0},{2,3},{3,2},{4,5},{5,4},{6,7},{7,6},{8,9},{9,8},{10,11... | collective-permute-start | bytes 786440 | tf_op jit(solution)/shard_map/ppermute | solution.py:763
  502.4 28.8 %collective-permute-start.49 = (bf16[128,1024]{1,0:T(8,128)(2,1)S(1)}, bf16[128,1024]{1,0:T(8,128)(2,1)S(1)}, u32[]{:S(2)}, u32[]{:S(2)}) collective-permute-start(bf16[128,1024]{1,0:T(8,128)(2,1)S(1)} %pad_maximum_fusion.7), channel_id=1, source_target_pairs={{0,8},{8,0},{16,24},{24,16},{1,9},{9,1},{17,25},{25,17},{2,10},{10... | collective-permute-start | bytes 786440 | tf_op jit(solution)/shard_map/ppermute | solution.py:763
  517.9 22.6 %collective-permute-start.22 = (bf16[2,2,64,1536]{3,2,1,0:T(8,128)(2,1)S(1)}, bf16[2,2,64,1536]{3,2,1,0:T(8,128)(2,1)S(1)}, u32[]{:S(2)}, u32[]{:S(2)}) collective-permute-start(bf16[2,2,64,1536]{3,2,1,0:T(8,128)(2,1)S(1)} %get-tuple-element.168), channel_id=1, source_target_pairs={{0,16},{8,24},{16,0},{24,8},{1,17},{9,25},{17,1},{25,9},{2,18},{10... | collective-permute-start | bytes 2359304 | tf_op jit(solution)/shard_map/ppermute | solution.py:763
  584.1 23.3 %collective-permute-start.26 = (bf16[128,1536]{1,0:T(8,128)(2,1)S(1)}, bf16[128,1536]{1,0:T(8,128)(2,1)S(1)}, u32[]{:S(2)}, u32[]{:S(2)}) collective-permute-start(bf16[128,1536]{1,0:T(8,128)(2,1)S(1)} %pad_maximum_fusion.5), channel_id=1, source_target_pairs={{0,8},{8,0},{16,24},{24,16},{1,9},{9,1},{17,25},{25,17},{2,10},{10... | collective-permute-start | bytes 1179656 | tf_op jit(solution)/shard_map/ppermute | solution.py:763
  (69 other events, 872.4 us)
